TPU v7x, 32 devices: a whole 2x2x4 slice. The times are simulated.
32 devices in a mesh: ctx: 16 (over z, y, x), fsdp: 2 (over core).
Axes of the slice: x: 2, y: 2, z: 4, core: 2. Of those that a mesh axis runs over, the one named last changes fastest.
Arguments:
- query_rows: bfloat16 [4096, 4096], P(('ctx', 'fsdp')), may hold values from -40 to 40
- key_rows: bfloat16 [4096, 512], P(('ctx', 'fsdp')), may hold values from -6 to 6
- value_matrix: bfloat16 [4096, 512], P(('ctx', 'fsdp')), may hold values from -6 to 6
- out_grad: bfloat16 [4096, 4096], P(('ctx', 'fsdp')), may hold values from -24 to 24
- segments: int32 [4096], P(('ctx', 'fsdp')), may hold values from 0 to 4, never falling along the last dimension, each value on 1 to 1536 neighbouring positions
Outputs:
- query_grad: bfloat16 [4096, 4096], P(('ctx', 'fsdp'))
- key_grad: bfloat16 [4096, 512], P(('ctx', 'fsdp'))
- value_grad: bfloat16 [4096, 512], P(('ctx', 'fsdp'))
Inputs may be any that keep to these rules, and one draw needn't show every extreme that they name: `segments`: segment numbers never fall along the sequence.
All inputs are finite; a program needn't handle non-finite values.
Results may differ from a plain program's by a relative error of at most 0.0085.
Values may be sent and summed in bfloat16 or wider, within the bound.
A program may use at most 64 MiB of HBM per device.

v0:
```python
import math

import jax
import jax.numpy as jnp
from jax import lax
from jax.sharding import PartitionSpec as P

HEAD_WIDTH = 128
SPAN = 3


def from_behind(block, axis, distance):
    devices = range(lax.axis_size(axis))
    route = [(i - distance, i) for i in devices if i - distance in devices]
    return lax.ppermute(block, axis, route)


def band_grads(
    query_blk, grad_blk, key_win, value_win, query_seg, key_seg, query_first, key_first, window
):
    tok_rows = query_blk.shape[0]
    key_count = key_win.shape[0]
    kv_heads = key_win.shape[1] // HEAD_WIDTH
    heads_per_group = query_blk.shape[1] // key_win.shape[1]
    inv_root = 1.0 / math.sqrt(HEAD_WIDTH)
    query_pos = query_first + jnp.arange(tok_rows, dtype=jnp.int32)
    key_pos = key_first + jnp.arange(key_count, dtype=jnp.int32)
    allowed = (key_pos[None, :] > query_pos[:, None] - window) & (
        key_pos[None, :] <= query_pos[:, None]
    )
    allowed = allowed & (key_pos[None, :] >= 0) & (key_seg[None, :] == query_seg[:, None])
    query_parts = []
    key_parts = []
    value_parts = []
    for kv_head in range(kv_heads):
        k_head = key_win[:, kv_head * HEAD_WIDTH : (kv_head + 1) * HEAD_WIDTH]
        v_head = value_win[:, kv_head * HEAD_WIDTH : (kv_head + 1) * HEAD_WIDTH]
        lower = kv_head * heads_per_group * HEAD_WIDTH
        q_head = query_blk[:, lower : lower + heads_per_group * HEAD_WIDTH].reshape(
            tok_rows, heads_per_group, HEAD_WIDTH
        )
        o_grad = grad_blk[:, lower : lower + heads_per_group * HEAD_WIDTH].reshape(
            tok_rows, heads_per_group, HEAD_WIDTH
        )
        scores = (
            jnp.einsum("trd,kd->rtk", q_head, k_head, preferred_element_type=jnp.float32) * inv_root
        )
        scores = jnp.where(allowed[None], scores, -1e30)
        row_max = jnp.max(scores, axis=-1, keepdims=True)
        weights = jnp.exp(scores - row_max)
        probs = weights / jnp.sum(weights, axis=-1, keepdims=True)
        prob_grad = jnp.einsum("trd,kd->rtk", o_grad, v_head, preferred_element_type=jnp.float32)
        row_delta = jnp.sum(probs * prob_grad, axis=-1, keepdims=True)
        score_grad = (probs * (prob_grad - row_delta) * inv_root).astype(jnp.bfloat16)
        probs_low = probs.astype(jnp.bfloat16)
        query_parts.append(
            jnp.einsum(
                "rtk,kd->trd", score_grad, k_head, preferred_element_type=jnp.float32
            ).reshape(tok_rows, heads_per_group * HEAD_WIDTH)
        )
        key_parts.append(
            jnp.einsum("rtk,trd->kd", score_grad, q_head, preferred_element_type=jnp.float32)
        )
        value_parts.append(
            jnp.einsum("rtk,trd->kd", probs_low, o_grad, preferred_element_type=jnp.float32)
        )
    return (
        jnp.concatenate(query_parts, 1),
        jnp.concatenate(key_parts, 1),
        jnp.concatenate(value_parts, 1),
    )


def body(query_rows, key_rows, value_matrix, out_grad, segments):
    tok_rows = query_rows.shape[0]
    position = lax.axis_index(("ctx", "fsdp"))
    query_first = position * tok_rows
    window = SPAN * tok_rows
    nearby = [(key_rows, value_matrix, segments)]
    for hop_back in range(1, SPAN + 1):
        nearby.insert(0, from_behind((key_rows, value_matrix, segments), ("ctx", "fsdp"), hop_back))
    key_win = jnp.concatenate([member[0] for member in nearby], 0)
    value_win = jnp.concatenate([member[1] for member in nearby], 0)
    seg_win = jnp.concatenate([member[2] for member in nearby], 0)
    dq_part, dk_part, dv_part = band_grads(
        query_rows,
        out_grad,
        key_win,
        value_win,
        segments,
        seg_win,
        query_first,
        query_first - window,
        window,
    )
    carried = (dk_part[:tok_rows], dv_part[:tok_rows])
    for relay_step in range(1, SPAN + 1):
        received = from_behind((carried[0], carried[1]), ("ctx", "fsdp"), -1)
        lower = relay_step * tok_rows
        carried = (
            received[0] + dk_part[lower : lower + tok_rows],
            received[1] + dv_part[lower : lower + tok_rows],
        )
    key_own = carried[0]
    value_own = carried[1]
    return (
        dq_part.astype(jnp.bfloat16),
        key_own.astype(jnp.bfloat16),
        value_own.astype(jnp.bfloat16),
    )


def solution(mesh):
    return jax.shard_map(
        body,
        mesh=mesh,
        in_specs=(
            P(("ctx", "fsdp"), None),
            P(("ctx", "fsdp"), None),
            P(("ctx", "fsdp"), None),
            P(("ctx", "fsdp"), None),
            P(("ctx", "fsdp")),
        ),
        out_specs=(P(("ctx", "fsdp"), None), P(("ctx", "fsdp"), None), P(("ctx", "fsdp"), None)),
        check_vma=False,
    )
```

profile of v0, /device:TPU:7, one launch (start us, length us, event | category | flops | bytes accessed | tf_op | source)
XLA Modules:
  0.0 134.1 jit_solution(4516723554598470065)
XLA Ops:
  0.6 3.8 %collective-permute-start.5 = (s32[128]{0:T(128)}, s32[128]{0:T(128)}, u32[]{:S(2)}, u32[]{:S(2)}) collective-permute-start(s32[128]{0:T(128)} %param.9), channel_id=1, source_target_pairs={{0,1},{1,2},{2,3},{3,4},{4,5},{5,6},{6,7},{7,8},{8,9},{9,10},{10,1... | collective-permute-start | bytes 1544 | tf_op jit(solution)/shard_map/ppermute | solution.py:15
  4.5 3.1 %collective-permute-start.4 = (s32[128]{0:T(128)}, s32[128]{0:T(128)}, u32[]{:S(2)}, u32[]{:S(2)}) collective-permute-start(s32[128]{0:T(128)} %param.9), channel_id=1, source_target_pairs={{0,2},{1,3},{2,4},{3,5},{4,6},{5,7},{6,8},{7,9},{8,10},{9,11},{10,... | collective-permute-start | bytes 1544 | tf_op jit(solution)/shard_map/ppermute | solution.py:15
  7.6 2.2 %collective-permute-start.3 = (s32[128]{0:T(128)}, s32[128]{0:T(128)}, u32[]{:S(2)}, u32[]{:S(2)}) collective-permute-start(s32[128]{0:T(128)} %param.9), channel_id=1, source_target_pairs={{0,3},{1,4},{2,5},{3,6},{4,7},{5,8},{6,9},{7,10},{8,11},{9,12},{10... | collective-permute-start | bytes 1544 | tf_op jit(solution)/shard_map/ppermute | solution.py:15
  9.8 3.1 %collective-permute-start.1 = (bf16[128,512]{1,0:T(8,128)(2,1)}, bf16[128,512]{1,0:T(8,128)(2,1)}, u32[]{:S(2)}, u32[]{:S(2)}) collective-permute-start(bf16[128,512]{1,0:T(8,128)(2,1)} %param.6), channel_id=1, source_target_pairs={{0,2},{1,3},{2,4},{3,5},{4,6},{5,7},{6,8},{7,9},{8,10},{9,11},{10,... | collective-permute-start | bytes 393224 | tf_op jit(solution)/shard_map/ppermute | solution.py:15
  13.0 4.6 %collective-permute-start = (bf16[128,512]{1,0:T(8,128)(2,1)}, bf16[128,512]{1,0:T(8,128)(2,1)}, u32[]{:S(2)}, u32[]{:S(2)}) collective-permute-start(bf16[128,512]{1,0:T(8,128)(2,1)} %param.6), channel_id=1, source_target_pairs={{0,3},{1,4},{2,5},{3,6},{4,7},{5,8},{6,9},{7,10},{8,11},{9,12},{10... | collective-permute-start | bytes 393224 | tf_op jit(solution)/shard_map/ppermute | solution.py:15
  18.1 1.3 fusion.86
  20.2 0.9 copy.108
  22.9 1.9 %collective-permute-start.2 = (bf16[128,512]{1,0:T(8,128)(2,1)S(1)}, bf16[128,512]{1,0:T(8,128)(2,1)S(1)}, u32[]{:S(2)}, u32[]{:S(2)}) collective-permute-start(bf16[128,512]{1,0:T(8,128)(2,1)S(1)} %copy-done.15), channel_id=1, source_target_pairs={{0,1},{1,2},{2,3},{3,4},{4,5},{5,6},{6,7},{7,8},{8,9},{9,10},{10,1... | collective-permute-start | bytes 393224 | tf_op jit(solution)/shard_map/ppermute | solution.py:15
  24.9 3.1 %collective-permute-start.7 = (bf16[128,512]{1,0:T(8,128)(2,1)S(1)}, bf16[128,512]{1,0:T(8,128)(2,1)S(1)}, u32[]{:S(2)}, u32[]{:S(2)}) collective-permute-start(bf16[128,512]{1,0:T(8,128)(2,1)S(1)} %copy-done.14), channel_id=1, source_target_pairs={{0,2},{1,3},{2,4},{3,5},{4,6},{5,7},{6,8},{7,9},{8,10},{9,11},{10,... | collective-permute-start | bytes 393224 | tf_op jit(solution)/shard_map/ppermute | solution.py:15
  28.0 3.8 %collective-permute-start.6 = (bf16[128,512]{1,0:T(8,128)(2,1)S(1)}, bf16[128,512]{1,0:T(8,128)(2,1)S(1)}, u32[]{:S(2)}, u32[]{:S(2)}) collective-permute-start(bf16[128,512]{1,0:T(8,128)(2,1)S(1)} %copy-done.14), channel_id=1, source_target_pairs={{0,3},{1,4},{2,5},{3,6},{4,7},{5,8},{6,9},{7,10},{8,11},{9,12},{10... | collective-permute-start | bytes 393224 | tf_op jit(solution)/shard_map/ppermute | solution.py:15
  32.5 0.9 compare_and_fusion
  33.5 1.7 %collective-permute-done.6 = bf16[128,512]{1,0:T(8,128)(2,1)S(1)} collective-permute-done((bf16[128,512]{1,0:T(8,128)(2,1)S(1)}, bf16[128,512]{1,0:T(8,128)(2,1)S(1)}, u32[]{:S(2)}, u32[]{:S(2)}) %collective-permute-start.6) | collective-permute-done | bytes 131104 | tf_op jit(solution)/shard_map/ppermute | solution.py:15
  35.1 4.2 %collective-permute-start.8 = (bf16[128,512]{1,0:T(8,128)(2,1)S(1)}, bf16[128,512]{1,0:T(8,128)(2,1)S(1)}, u32[]{:S(2)}, u32[]{:S(2)}) collective-permute-start(bf16[128,512]{1,0:T(8,128)(2,1)S(1)} %copy-done.14), channel_id=1, source_target_pairs={{0,1},{1,2},{2,3},{3,4},{4,5},{5,6},{6,7},{7,8},{8,9},{9,10},{10,1... | collective-permute-start | bytes 393224 | tf_op jit(solution)/shard_map/ppermute | solution.py:15
  39.4 1.9 %collective-permute-done.8 = bf16[128,512]{1,0:T(8,128)(2,1)S(1)} collective-permute-done((bf16[128,512]{1,0:T(8,128)(2,1)S(1)}, bf16[128,512]{1,0:T(8,128)(2,1)S(1)}, u32[]{:S(2)}, u32[]{:S(2)}) %collective-permute-start.8) | collective-permute-done | bytes 131104 | tf_op jit(solution)/shard_map/ppermute | solution.py:15
  41.3 1.1 constant_dynamic-update-slice_fusion.3
  42.4 0.9 constant_dynamic-update-slice_fusion.2
  44.6 3.0 %fusion.88 = (f32[8,128]{1,0:T(8,128)S(1)}, f32[8,128,512]{1,2,0:T(8,128)}) fusion(pred[128,512]{0,1:T(8,128)(4,1)} %compare_and_fusion, bf16[128,8,128]{0,2,1:T(8,128)(2,1)S(1)} %bitcast.265, bf16[512,512]{1,0:T(8,128)(2,1)} %copy-done.17), kind=kOutput, calls=%fused_computation.147 | convolution fusion | flops 136315392 | bytes 2560000 | tf_op jit(solution)/shard_map/sub | solution.py:50
  47.7 2.8 %convolution_bitcast_fusion = f32[512,128]{0,1:T(8,128)} fusion(bf16[128,8,128]{0,2,1:T(8,128)(2,1)S(1)} %bitcast.255, f32[8,128]{1,0:T(8,128)S(1)} %get-tuple-element.17, pred[128,512]{0,1:T(8,128)(4,1)S(1)} %copy-done.16, bf16[128,8,128]{0,2,1:T(8,128)(2,1)S(1)} %bitcast.266, bf16[512,512]{1,0:T(8,128)(2,1)} %copy-done.17), kind=kOutput, calls=%fused_computation.44 | convolution fusion | flops 271058432 | bytes 987136 | tf_op jit(solution)/shard_map/rtk,trd->kd/dot_general | solution.py:65
  50.4 3.7 %convolution_bitcast_fusion.4 = f32[512,128]{0,1:T(8,128)} fusion(bf16[128,8,128]{0,2,1:T(8,128)(2,1)S(1)} %bitcast.267, f32[512,128,8]{1,0,2:T(8,128)S(1)} %fusion.54, f32[8,128,512]{1,2,0:T(8,128)} %get-tuple-element.18, f32[8,128]{1,0:T(8,128)S(1)} %get-tuple-element.17), kind=kOutput, calls=%fused_computation.48 | convolution fusion | flops 137889280 | bytes 4722688 | tf_op jit(solution)/shard_map/rtk,trd->kd/dot_general | solution.py:62
  54.2 3.8 %convolution_convert_fusion = bf16[128,8,128]{2,0,1:T(8,128)(2,1)} fusion(f32[512,128,8]{1,0,2:T(8,128)S(1)} %fusion.54, bf16[512,512]{1,0:T(8,128)(2,1)} %copy-done.17, f32[8,128,512]{1,2,0:T(8,128)} %get-tuple-element.18, f32[8,128]{1,0:T(8,128)S(1)} %get-tuple-element.17), kind=kOutput, calls=%fused_computation.40 | convolution fusion | flops 138020352 | bytes 8790016 | tf_op jit(solution)/shard_map/rtk,kd->trd/dot_general | solution.py:57
  58.4 3.1 %fusion.90 = (f32[8,128]{1,0:T(8,128)S(1)}, f32[8,128,512]{1,2,0:T(8,128)}) fusion(pred[128,512]{0,1:T(8,128)(4,1)S(1)} %copy-done.16, bf16[128,8,128]{0,2,1:T(8,128)(2,1)} %bitcast.262, bf16[512,512]{1,0:T(8,128)(2,1)} %copy-done.17), kind=kOutput, calls=%fused_computation.149 | convolution fusion | flops 136315392 | bytes 2560000 | tf_op jit(solution)/shard_map/sub | solution.py:50
  61.5 2.9 %convolution_bitcast_fusion.2 = f32[512,128]{0,1:T(8,128)} fusion(bf16[128,8,128]{0,2,1:T(8,128)(2,1)S(1)} %bitcast.253, f32[8,128]{1,0:T(8,128)S(1)} %get-tuple-element.21, pred[128,512]{0,1:T(8,128)(4,1)S(1)} %copy-done.16, bf16[128,8,128]{0,2,1:T(8,128)(2,1)} %bitcast.263, bf16[512,512]{1,0:T(8,128)(2,1)} %copy-done.17), kind=kOutput, calls=%fused_computation.46 | convolution fusion | flops 271058432 | bytes 987136 | tf_op jit(solution)/shard_map/rtk,trd->kd/dot_general | solution.py:65
  64.4 3.7 %convolution_bitcast_fusion.6 = f32[512,128]{0,1:T(8,128)} fusion(bf16[128,8,128]{0,2,1:T(8,128)(2,1)} %bitcast.264, f32[512,128,8]{1,0,2:T(8,128)S(1)} %fusion.56, f32[8,128,512]{1,2,0:T(8,128)} %get-tuple-element.22, f32[8,128]{1,0:T(8,128)S(1)} %get-tuple-element.21), kind=kOutput, calls=%fused_computation.50 | convolution fusion | flops 137889280 | bytes 4722688 | tf_op jit(solution)/shard_map/rtk,trd->kd/dot_general | solution.py:62
  68.1 3.8 %convolution_convert_fusion.2 = bf16[128,8,128]{2,0,1:T(8,128)(2,1)} fusion(f32[512,128,8]{1,0,2:T(8,128)S(1)} %fusion.56, bf16[512,512]{1,0:T(8,128)(2,1)} %copy-done.17, f32[8,128,512]{1,2,0:T(8,128)} %get-tuple-element.22, f32[8,128]{1,0:T(8,128)S(1)} %get-tuple-element.21), kind=kOutput, calls=%fused_computation.42 | convolution fusion | flops 138020352 | bytes 8790016 | tf_op jit(solution)/shard_map/rtk,kd->trd/dot_general | solution.py:57
  71.9 1.8 %fusion.55 = f32[512,128,8]{1,0,2:T(8,128)} fusion(bf16[128,8,128]{0,2,1:T(8,128)(2,1)S(1)} %bitcast.250, bf16[512,512]{1,0:T(8,128)(2,1)S(1)} %copy-done.3), kind=kOutput, calls=%fused_computation.96 | convolution fusion | flops 134217728 | bytes 2490368 | tf_op jit(solution)/shard_map/trd,kd->rtk/dot_general | solution.py:52
  74.1 3.3 %fusion.89 = (f32[8,128]{1,0:T(8,128)S(1)}, f32[8,128,512]{1,2,0:T(8,128)}) fusion(pred[128,512]{0,1:T(8,128)(4,1)S(1)} %copy-done.16, bf16[128,8,128]{0,2,1:T(8,128)(2,1)S(1)} %bitcast.259, bf16[512,512]{1,0:T(8,128)(2,1)} %copy-done.17), kind=kOutput, calls=%fused_computation.148 | convolution fusion | flops 136315392 | bytes 2560000 | tf_op jit(solution)/shard_map/sub | solution.py:50
  77.4 2.1 %convolution_bitcast_fusion.1 = f32[512,128]{0,1:T(8,128)S(1)} fusion(bf16[128,8,128]{0,2,1:T(8,128)(2,1)S(1)} %bitcast.251, f32[8,128]{1,0:T(8,128)S(1)} %get-tuple-element.19, pred[128,512]{0,1:T(8,128)(4,1)S(1)} %copy-done.16, bf16[128,8,128]{0,2,1:T(8,128)(2,1)S(1)} %bitcast.260, bf16[512,512]{1,0:T(8,128)(2,1)} %copy-done.17), kind=kOutput, calls=%fused_computation.45 | convolution fusion | flops 271058432 | bytes 987136 | tf_op jit(solution)/shard_map/rtk,trd->kd/dot_general | solution.py:65
  79.5 3.0 %fusion.91 = (f32[8,128]{1,0:T(8,128)S(1)}, f32[8,128,512]{1,2,0:T(8,128)}) fusion(pred[128,512]{0,1:T(8,128)(4,1)S(1)} %copy-done.16, bf16[128,8,128]{0,2,1:T(8,128)(2,1)S(1)} %bitcast.256, bf16[512,512]{1,0:T(8,128)(2,1)} %copy-done.17), kind=kOutput, calls=%fused_computation.150 | convolution fusion | flops 136315392 | bytes 2560000 | tf_op jit(solution)/shard_map/sub | solution.py:50
  82.5 2.8 %convolution_bitcast_fusion.3 = f32[512,128]{0,1:T(8,128)} fusion(bf16[128,8,128]{0,2,1:T(8,128)(2,1)S(1)} %bitcast.249, f32[8,128]{1,0:T(8,128)S(1)} %get-tuple-element.23, pred[128,512]{0,1:T(8,128)(4,1)S(1)} %copy-done.16, bf16[128,8,128]{0,2,1:T(8,128)(2,1)S(1)} %bitcast.257, bf16[512,512]{1,0:T(8,128)(2,1)} %copy-done.17), kind=kOutput, calls=%fused_computation.47 | convolution fusion | flops 271058432 | bytes 987136 | tf_op jit(solution)/shard_map/rtk,trd->kd/dot_general | solution.py:65
  85.2 5.0 %convolution_bitcast_fusion.5 = f32[512,128]{0,1:T(8,128)} fusion(bf16[128,8,128]{0,2,1:T(8,128)(2,1)S(1)} %bitcast.261, f32[512,128,8]{1,0,2:T(8,128)} %fusion.55, f32[8,128,512]{1,2,0:T(8,128)} %get-tuple-element.20, f32[8,128]{1,0:T(8,128)S(1)} %get-tuple-element.19), kind=kOutput, calls=%fused_computation.49 | convolution fusion | flops 137889280 | bytes 4722688 | tf_op jit(solution)/shard_map/rtk,trd->kd/dot_general | solution.py:62
  90.2 4.0 %convolution_bitcast_fusion.7 = f32[512,128]{0,1:T(8,128)} fusion(bf16[128,8,128]{0,2,1:T(8,128)(2,1)S(1)} %bitcast.258, f32[512,128,8]{1,0,2:T(8,128)S(1)} %fusion.57, f32[8,128,512]{1,2,0:T(8,128)} %get-tuple-element.24, f32[8,128]{1,0:T(8,128)S(1)} %get-tuple-element.23), kind=kOutput, calls=%fused_computation.51 | convolution fusion | flops 137889280 | bytes 4722688 | tf_op jit(solution)/shard_map/rtk,trd->kd/dot_general | solution.py:62
  94.2 1.2 pad_maximum_fusion.1
  95.4 2.2 %collective-permute-start.9 = (f32[128,512]{0,1:T(8,128)S(1)}, f32[128,512]{0,1:T(8,128)S(1)}, u32[]{:S(2)}, u32[]{:S(2)}) collective-permute-start(f32[128,512]{0,1:T(8,128)S(1)} %slice.104), channel_id=1, source_target_pairs={{1,0},{2,1},{3,2},{4,3},{5,4},{6,5},{7,6},{8,7},{9,8},{10,9},{11,1... | collective-permute-start | bytes 786440 | tf_op jit(solution)/shard_map/ppermute | solution.py:15
  98.5 1.9 %collective-permute-start.12 = (f32[128,512]{0,1:T(8,128)}, f32[128,512]{0,1:T(8,128)S(1)}, u32[]{:S(2)}, u32[]{:S(2)}) collective-permute-start(f32[128,512]{0,1:T(8,128)} %slice.108), channel_id=1, source_target_pairs={{1,0},{2,1},{3,2},{4,3},{5,4},{6,5},{7,6},{8,7},{9,8},{10,9},{11,1... | collective-permute-start | bytes 786440 | tf_op jit(solution)/shard_map/ppermute | solution.py:15
  100.4 4.3 %convolution_convert_fusion.1 = bf16[128,8,128]{2,0,1:T(8,128)(2,1)S(1)} fusion(f32[512,128,8]{1,0,2:T(8,128)} %fusion.55, bf16[512,512]{1,0:T(8,128)(2,1)} %copy-done.17, f32[8,128,512]{1,2,0:T(8,128)} %get-tuple-element.20, f32[8,128]{1,0:T(8,128)S(1)} %get-tuple-element.19), kind=kOutput, calls=%fused_computation.41 | convolution fusion | flops 138020352 | bytes 8790016 | tf_op jit(solution)/shard_map/rtk,kd->trd/dot_general | solution.py:57
  104.7 0.9 collective-permute-done.9
  105.6 3.7 %collective-permute-start.10 = (f32[128,512]{0,1:T(8,128)S(1)}, f32[128,512]{0,1:T(8,128)}, u32[]{:S(2)}, u32[]{:S(2)}) collective-permute-start(f32[128,512]{0,1:T(8,128)S(1)} %slice_add_fusion.5), channel_id=1, source_target_pairs={{1,0},{2,1},{3,2},{4,3},{5,4},{6,5},{7,6},{8,7},{9,8},{10,9},{11,1... | collective-permute-start | bytes 786440 | tf_op jit(solution)/shard_map/ppermute | solution.py:15
  110.2 2.0 %collective-permute-start.13 = (f32[128,512]{0,1:T(8,128)}, f32[128,512]{0,1:T(8,128)}, u32[]{:S(2)}, u32[]{:S(2)}) collective-permute-start(f32[128,512]{0,1:T(8,128)} %slice_add_fusion.2), channel_id=1, source_target_pairs={{1,0},{2,1},{3,2},{4,3},{5,4},{6,5},{7,6},{8,7},{9,8},{10,9},{11,1... | collective-permute-start | bytes 786440 | tf_op jit(solution)/shard_map/ppermute | solution.py:15
  112.2 5.0 %convolution_convert_fusion.3 = bf16[128,8,128]{2,0,1:T(8,128)(2,1)} fusion(f32[512,128,8]{1,0,2:T(8,128)} %copy-done, bf16[512,512]{1,0:T(8,128)(2,1)} %copy-done.17, f32[8,128,512]{1,2,0:T(8,128)} %get-tuple-element.24, f32[8,128]{1,0:T(8,128)S(1)} %get-tuple-element.23), kind=kOutput, calls=%fused_computation.43 | convolution fusion | flops 138020352 | bytes 8790016 | tf_op jit(solution)/shard_map/rtk,kd->trd/dot_general | solution.py:57
  117.7 1.1 copy.62
  118.8 1.0 slice_add_fusion.4
  119.8 1.9 %collective-permute-start.11 = (f32[128,512]{0,1:T(8,128)S(1)}, f32[128,512]{0,1:T(8,128)S(1)}, u32[]{:S(2)}, u32[]{:S(2)}) collective-permute-start(f32[128,512]{0,1:T(8,128)S(1)} %slice_add_fusion.4), channel_id=1, source_target_pairs={{1,0},{2,1},{3,2},{4,3},{5,4},{6,5},{7,6},{8,7},{9,8},{10,9},{11,1... | collective-permute-start | bytes 786440 | tf_op jit(solution)/shard_map/ppermute | solution.py:15
  121.7 1.0 slice_add_fusion.1
  122.7 1.9 %collective-permute-start.14 = (f32[128,512]{0,1:T(8,128)S(1)}, f32[128,512]{0,1:T(8,128)}, u32[]{:S(2)}, u32[]{:S(2)}) collective-permute-start(f32[128,512]{0,1:T(8,128)S(1)} %slice_add_fusion.1), channel_id=1, source_target_pairs={{1,0},{2,1},{3,2},{4,3},{5,4},{6,5},{7,6},{8,7},{9,8},{10,9},{11,1... | collective-permute-start | bytes 786440 | tf_op jit(solution)/shard_map/ppermute | solution.py:15
  124.6 1.0 pad_maximum_fusion
  125.7 3.6 %collective-permute-done.11 = f32[128,512]{0,1:T(8,128)S(1)} collective-permute-done((f32[128,512]{0,1:T(8,128)S(1)}, f32[128,512]{0,1:T(8,128)S(1)}, u32[]{:S(2)}, u32[]{:S(2)}) %collective-permute-start.11) | collective-permute-done | bytes 262176 | tf_op jit(solution)/shard_map/ppermute | solution.py:15
  130.1 2.2 %collective-permute-done.14 = f32[128,512]{0,1:T(8,128)} collective-permute-done((f32[128,512]{0,1:T(8,128)S(1)}, f32[128,512]{0,1:T(8,128)}, u32[]{:S(2)}, u32[]{:S(2)}) %collective-permute-start.14) | collective-permute-done | bytes 262176 | tf_op jit(solution)/shard_map/ppermute | solution.py:15
  132.3 1.0 fusion.44
  (82 shorter events, 9.7 us)
Async XLA Ops:
  0.6 21.3 %copy-start.1 = (bf16[128,4096]{1,0:T(8,128)(2,1)S(1)}, bf16[128,4096]{1,0:T(8,128)(2,1)}, u32[]{:S(2)}) copy-start(bf16[128,4096]{1,0:T(8,128)(2,1)} %param.8) | copy-start | bytes 3145732
  0.6 22.3 %collective-permute-start.5 = (s32[128]{0:T(128)}, s32[128]{0:T(128)}, u32[]{:S(2)}, u32[]{:S(2)}) collective-permute-start(s32[128]{0:T(128)} %param.9), channel_id=1, source_target_pairs={{0,1},{1,2},{2,3},{3,4},{4,5},{5,6},{6,7},{7,8},{8,9},{9,10},{10,1... | collective-permute-start | bytes 1544 | tf_op jit(solution)/shard_map/ppermute | solution.py:15
  4.5 20.4 %collective-permute-start.4 = (s32[128]{0:T(128)}, s32[128]{0:T(128)}, u32[]{:S(2)}, u32[]{:S(2)}) collective-permute-start(s32[128]{0:T(128)} %param.9), channel_id=1, source_target_pairs={{0,2},{1,3},{2,4},{3,5},{4,6},{5,7},{6,8},{7,9},{8,10},{9,11},{10,... | collective-permute-start | bytes 1544 | tf_op jit(solution)/shard_map/ppermute | solution.py:15
  7.6 20.4 %collective-permute-start.3 = (s32[128]{0:T(128)}, s32[128]{0:T(128)}, u32[]{:S(2)}, u32[]{:S(2)}) collective-permute-start(s32[128]{0:T(128)} %param.9), channel_id=1, source_target_pairs={{0,3},{1,4},{2,5},{3,6},{4,7},{5,8},{6,9},{7,10},{8,11},{9,12},{10... | collective-permute-start | bytes 1544 | tf_op jit(solution)/shard_map/ppermute | solution.py:15
  9.8 32.6 %collective-permute-start.1 = (bf16[128,512]{1,0:T(8,128)(2,1)}, bf16[128,512]{1,0:T(8,128)(2,1)}, u32[]{:S(2)}, u32[]{:S(2)}) collective-permute-start(bf16[128,512]{1,0:T(8,128)(2,1)} %param.6), channel_id=1, source_target_pairs={{0,2},{1,3},{2,4},{3,5},{4,6},{5,7},{6,8},{7,9},{8,10},{9,11},{10,... | collective-permute-start | bytes 393224 | tf_op jit(solution)/shard_map/ppermute | solution.py:15
  13.0 28.4 %collective-permute-start = (bf16[128,512]{1,0:T(8,128)(2,1)}, bf16[128,512]{1,0:T(8,128)(2,1)}, u32[]{:S(2)}, u32[]{:S(2)}) collective-permute-start(bf16[128,512]{1,0:T(8,128)(2,1)} %param.6), channel_id=1, source_target_pairs={{0,3},{1,4},{2,5},{3,6},{4,7},{5,8},{6,9},{7,10},{8,11},{9,12},{10... | collective-permute-start | bytes 393224 | tf_op jit(solution)/shard_map/ppermute | solution.py:15
  21.9 3.0 %copy-start.14 = (bf16[128,512]{1,0:T(8,128)(2,1)S(1)}, bf16[128,512]{1,0:T(8,128)(2,1)}, u32[]{:S(2)}) copy-start(bf16[128,512]{1,0:T(8,128)(2,1)} %param.7) | copy-start | bytes 393220
  21.9 9.9 %copy-start.18 = (s32[128]{0:T(128)S(1)}, s32[128]{0:T(128)}, u32[]{:S(2)}) copy-start(s32[128]{0:T(128)} %param.9) | copy-start | bytes 1540
  22.0 0.9 copy-start.15
  22.0 10.5 %copy-start.19 = (pred[512]{0:T(512)(128)(4,1)S(1)}, pred[512]{0:T(512)(128)(4,1)}, u32[]{:S(2)}) copy-start(pred[512]{0:T(512)(128)(4,1)} %broadcast_compare_fusion) | copy-start | bytes 1540
  22.9 20.4 %collective-permute-start.2 = (bf16[128,512]{1,0:T(8,128)(2,1)S(1)}, bf16[128,512]{1,0:T(8,128)(2,1)S(1)}, u32[]{:S(2)}, u32[]{:S(2)}) collective-permute-start(bf16[128,512]{1,0:T(8,128)(2,1)S(1)} %copy-done.15), channel_id=1, source_target_pairs={{0,1},{1,2},{2,3},{3,4},{4,5},{5,6},{6,7},{7,8},{8,9},{9,10},{10,1... | collective-permute-start | bytes 393224 | tf_op jit(solution)/shard_map/ppermute | solution.py:15
  24.9 14.5 %collective-permute-start.7 = (bf16[128,512]{1,0:T(8,128)(2,1)S(1)}, bf16[128,512]{1,0:T(8,128)(2,1)S(1)}, u32[]{:S(2)}, u32[]{:S(2)}) collective-permute-start(bf16[128,512]{1,0:T(8,128)(2,1)S(1)} %copy-done.14), channel_id=1, source_target_pairs={{0,2},{1,3},{2,4},{3,5},{4,6},{5,7},{6,8},{7,9},{8,10},{9,11},{10,... | collective-permute-start | bytes 393224 | tf_op jit(solution)/shard_map/ppermute | solution.py:15
  28.0 7.1 %collective-permute-start.6 = (bf16[128,512]{1,0:T(8,128)(2,1)S(1)}, bf16[128,512]{1,0:T(8,128)(2,1)S(1)}, u32[]{:S(2)}, u32[]{:S(2)}) collective-permute-start(bf16[128,512]{1,0:T(8,128)(2,1)S(1)} %copy-done.14), channel_id=1, source_target_pairs={{0,3},{1,4},{2,5},{3,6},{4,7},{5,8},{6,9},{7,10},{8,11},{9,12},{10... | collective-permute-start | bytes 393224 | tf_op jit(solution)/shard_map/ppermute | solution.py:15
  35.1 6.2 %collective-permute-start.8 = (bf16[128,512]{1,0:T(8,128)(2,1)S(1)}, bf16[128,512]{1,0:T(8,128)(2,1)S(1)}, u32[]{:S(2)}, u32[]{:S(2)}) collective-permute-start(bf16[128,512]{1,0:T(8,128)(2,1)S(1)} %copy-done.14), channel_id=1, source_target_pairs={{0,1},{1,2},{2,3},{3,4},{4,5},{5,6},{6,7},{7,8},{8,9},{9,10},{10,1... | collective-permute-start | bytes 393224 | tf_op jit(solution)/shard_map/ppermute | solution.py:15
  41.3 2.9 %copy-start.2 = (bf16[512,512]{1,0:T(8,128)(2,1)}, bf16[512,512]{1,0:T(8,128)(2,1)S(1)}, u32[]{:S(2)}) copy-start(bf16[512,512]{1,0:T(8,128)(2,1)S(1)} %constant_dynamic-update-slice_fusion.4) | copy-start | bytes 1572868
  43.4 0.8 copy-start.17
  44.6 3.1 %copy-start.16 = (pred[128,512]{0,1:T(8,128)(4,1)S(1)}, pred[128,512]{0,1:T(8,128)(4,1)}, u32[]{:S(2)}) copy-start(pred[128,512]{0,1:T(8,128)(4,1)} %compare_and_fusion) | copy-start | bytes 196612
  54.2 3.8 %copy-start.3 = (bf16[512,512]{1,0:T(8,128)(2,1)S(1)}, bf16[512,512]{1,0:T(8,128)(2,1)}, u32[]{:S(2)}) copy-start(bf16[512,512]{1,0:T(8,128)(2,1)} %copy-done.2) | copy-start | bytes 1572868
  71.9 2.2 %copy-start.5 = (bf16[128,1024]{0,1:T(8,128)(2,1)S(1)}, bf16[128,1024]{0,1:T(8,128)(2,1)}, u32[]{:S(2)}) copy-start(bf16[128,1024]{0,1:T(8,128)(2,1)} %copy.108) | copy-start | bytes 786436
  74.1 16.1 %copy-start = (f32[512,128,8]{1,0,2:T(8,128)}, f32[512,128,8]{1,0,2:T(8,128)S(1)}, u32[]{:S(2)}) copy-start(f32[512,128,8]{1,0,2:T(8,128)S(1)} %fusion.57) | copy-start | bytes 6291460
  74.1 3.3 %copy-start.6 = (bf16[128,1024]{0,1:T(8,128)(2,1)S(1)}, bf16[128,1024]{0,1:T(8,128)(2,1)}, u32[]{:S(2)}) copy-start(bf16[128,1024]{0,1:T(8,128)(2,1)} %copy.108) | copy-start | bytes 786436
  77.4 2.1 %copy-start.4 = (bf16[128,1024]{0,1:T(8,128)(2,1)S(1)}, bf16[128,1024]{0,1:T(8,128)(2,1)}, u32[]{:S(2)}) copy-start(bf16[128,1024]{0,1:T(8,128)(2,1)} %copy.104) | copy-start | bytes 786436
  90.2 4.0 %copy-start.11 = (f32[512,128]{0,1:T(8,128)S(1)}, f32[512,128]{0,1:T(8,128)}, u32[]{:S(2)}) copy-start(f32[512,128]{0,1:T(8,128)} %convolution_bitcast_fusion.4) | copy-start | bytes 786436
  90.2 4.0 %copy-start.12 = (f32[512,128]{0,1:T(8,128)S(1)}, f32[512,128]{0,1:T(8,128)}, u32[]{:S(2)}) copy-start(f32[512,128]{0,1:T(8,128)} %convolution_bitcast_fusion.6) | copy-start | bytes 786436
  94.1 3.5 %copy-start.9 = (f32[512,128]{0,1:T(8,128)S(1)}, f32[512,128]{0,1:T(8,128)}, u32[]{:S(2)}) copy-start(f32[512,128]{0,1:T(8,128)} %convolution_bitcast_fusion) | copy-start | bytes 786436
  94.2 3.5 %copy-start.10 = (f32[512,128]{0,1:T(8,128)S(1)}, f32[512,128]{0,1:T(8,128)}, u32[]{:S(2)}) copy-start(f32[512,128]{0,1:T(8,128)} %convolution_bitcast_fusion.2) | copy-start | bytes 786436
  94.2 3.5 %copy-start.13 = (f32[512,128]{0,1:T(8,128)S(1)}, f32[512,128]{0,1:T(8,128)}, u32[]{:S(2)}) copy-start(f32[512,128]{0,1:T(8,128)} %convolution_bitcast_fusion.3) | copy-start | bytes 786436
  95.4 10.2 %collective-permute-start.9 = (f32[128,512]{0,1:T(8,128)S(1)}, f32[128,512]{0,1:T(8,128)S(1)}, u32[]{:S(2)}, u32[]{:S(2)}) collective-permute-start(f32[128,512]{0,1:T(8,128)S(1)} %slice.104), channel_id=1, source_target_pairs={{1,0},{2,1},{3,2},{4,3},{5,4},{6,5},{7,6},{8,7},{9,8},{10,9},{11,1... | collective-permute-start | bytes 786440 | tf_op jit(solution)/shard_map/ppermute | solution.py:15
  98.5 10.9 %collective-permute-start.12 = (f32[128,512]{0,1:T(8,128)}, f32[128,512]{0,1:T(8,128)S(1)}, u32[]{:S(2)}, u32[]{:S(2)}) collective-permute-start(f32[128,512]{0,1:T(8,128)} %slice.108), channel_id=1, source_target_pairs={{1,0},{2,1},{3,2},{4,3},{5,4},{6,5},{7,6},{8,7},{9,8},{10,9},{11,1... | collective-permute-start | bytes 786440 | tf_op jit(solution)/shard_map/ppermute | solution.py:15
  105.6 13.1 %collective-permute-start.10 = (f32[128,512]{0,1:T(8,128)S(1)}, f32[128,512]{0,1:T(8,128)}, u32[]{:S(2)}, u32[]{:S(2)}) collective-permute-start(f32[128,512]{0,1:T(8,128)S(1)} %slice_add_fusion.5), channel_id=1, source_target_pairs={{1,0},{2,1},{3,2},{4,3},{5,4},{6,5},{7,6},{8,7},{9,8},{10,9},{11,1... | collective-permute-start | bytes 786440 | tf_op jit(solution)/shard_map/ppermute | solution.py:15
  110.1 7.0 %copy-start.7 = (bf16[128,8,128]{2,0,1:T(8,128)(2,1)S(1)}, bf16[128,8,128]{2,0,1:T(8,128)(2,1)}, u32[]{:S(2)}) copy-start(bf16[128,8,128]{2,0,1:T(8,128)(2,1)} %convolution_convert_fusion) | copy-start | bytes 786436
  110.2 7.2 %copy-start.8 = (bf16[128,8,128]{2,0,1:T(8,128)(2,1)S(1)}, bf16[128,8,128]{2,0,1:T(8,128)(2,1)}, u32[]{:S(2)}) copy-start(bf16[128,8,128]{2,0,1:T(8,128)(2,1)} %convolution_convert_fusion.2) | copy-start | bytes 786436
  110.2 11.5 %collective-permute-start.13 = (f32[128,512]{0,1:T(8,128)}, f32[128,512]{0,1:T(8,128)}, u32[]{:S(2)}, u32[]{:S(2)}) collective-permute-start(f32[128,512]{0,1:T(8,128)} %slice_add_fusion.2), channel_id=1, source_target_pairs={{1,0},{2,1},{3,2},{4,3},{5,4},{6,5},{7,6},{8,7},{9,8},{10,9},{11,1... | collective-permute-start | bytes 786440 | tf_op jit(solution)/shard_map/ppermute | solution.py:15
  119.8 9.5 %collective-permute-start.11 = (f32[128,512]{0,1:T(8,128)S(1)}, f32[128,512]{0,1:T(8,128)S(1)}, u32[]{:S(2)}, u32[]{:S(2)}) collective-permute-start(f32[128,512]{0,1:T(8,128)S(1)} %slice_add_fusion.4), channel_id=1, source_target_pairs={{1,0},{2,1},{3,2},{4,3},{5,4},{6,5},{7,6},{8,7},{9,8},{10,9},{11,1... | collective-permute-start | bytes 786440 | tf_op jit(solution)/shard_map/ppermute | solution.py:15
  122.7 9.6 %collective-permute-start.14 = (f32[128,512]{0,1:T(8,128)S(1)}, f32[128,512]{0,1:T(8,128)}, u32[]{:S(2)}, u32[]{:S(2)}) collective-permute-start(f32[128,512]{0,1:T(8,128)S(1)} %slice_add_fusion.1), channel_id=1, source_target_pairs={{1,0},{2,1},{3,2},{4,3},{5,4},{6,5},{7,6},{8,7},{9,8},{10,9},{11,1... | collective-permute-start | bytes 786440 | tf_op jit(solution)/shard_map/ppermute | solution.py:15
where the time goes:
time: 136 us; the launch traced here: 134 us
  matrix products  59.1 us (43%)
  starting transfers between devices  43.7 us (32%)
  local copies, waits for them, and re-layouts  11.5 us (8%)
  waiting for transfers between devices  10.3 us (8%)
  other arithmetic  8.22 us (6%)
    ppermute x15, starting transfers between devices, from_behind(): return lax.ppermute(block, axis, route)  43.7 us
    dot_general x4, matrix products, band_grads(): jnp.einsum('rtk,kd->trd', score_grad, k_head, preferred_element_type=jnp....  16.8 us
    dot_general x4, matrix products, band_grads(): jnp.einsum('rtk,trd->kd', score_grad, q_head, preferred_element_type=jnp....  16.4 us
    sub x4, matrix products, band_grads(): weights = jnp.exp(scores - row_max)  12.4 us
    dot_general x4, matrix products, band_grads(): jnp.einsum('rtk,trd->kd', probs_low, o_grad, preferred_element_type=jnp.f...  10.5 us
    ppermute x15, waiting for transfers between devices, from_behind(): return lax.ppermute(block, axis, route)  10.3 us
    unnamed x56, local copies, waits for them, and re-layouts  7.85 us
    dot_general x4, matrix products, band_grads(): jnp.einsum('trd,kd->rtk', o_grad, v_head, preferred_element_type=jnp.floa...  3.01 us
  transfers between devices with their start and end apart: 15, of which 5 were waited for; matrix products, arithmetic and copies ran while one was open for 19% of the time, Pallas kernels for 0%

commit v1 on v0

v1 whole, which is shorter than its diff:
```python
import functools
import math

import jax
import jax.numpy as jnp
from jax import lax
from jax.experimental import pallas as pl
from jax.experimental.pallas import tpu as pltpu
from jax.sharding import PartitionSpec as P

HEAD = 128
GROUP = 8
TOK = 128
SLOTS = 5
WIDE = GROUP * HEAD
INV_ROOT = 1.0 / math.sqrt(HEAD)
TO_EXP2 = INV_ROOT * math.log2(math.e)
MESH = pl.DeviceIdType.MESH
NT = (((1,), (1,)), ((), ()))


def kernel(
    inner, count,
    q_in, k_in, v_in, o_in, seg_in,
    dq_out, dk_out, dv_out,
    qb, ob, kw, vw, segw, bias, pb, sb, dqs, acc_k, acc_v, stage, back,
    local_sem, seg_send, seg_recv, kv_send, kv_recv, q_send, q_recv,
    dq_sem, dq_recv, back_send, back_recv,
):
    pos = lax.axis_index("ctx") * inner + lax.axis_index("fsdp")
    pairs = count // 2
    pair, core = pos // 2, pos % 2
    other = 1 - core

    def place(p):
        return (p // inner, p % inner)

    partner = 2 * pair + other
    has_next = pair + 1 < pairs
    has_next2 = jnp.logical_and(core == 1, pair + 2 < pairs)
    has_prev = pair >= 1
    has_prev2 = pair >= 2

    def kv_cols(h):
        return pl.ds(pl.multiple_of(h * HEAD, HEAD), HEAD)

    def q_cols(h):
        return pl.ds(pl.multiple_of(h * WIDE, WIDE), WIDE)

    own = []
    for gl in range(2):
        h = 2 * core + gl
        own.append(
            (
                pltpu.make_async_copy(k_in.at[:, kv_cols(h)], kw.at[gl, 3 + core], local_sem.at[0, gl]),
                pltpu.make_async_copy(v_in.at[:, kv_cols(h)], vw.at[gl, 3 + core], local_sem.at[1, gl]),
                pltpu.make_async_copy(q_in.at[:, q_cols(h)], qb.at[gl, core], local_sem.at[2, gl]),
                pltpu.make_async_copy(o_in.at[:, q_cols(h)], ob.at[gl, core], local_sem.at[3, gl]),
            )
        )

    barrier = pltpu.get_barrier_semaphore()

    def greet(p):
        pl.semaphore_signal(barrier, inc=1, device_id=place(p), device_id_type=MESH)

    greet(partner)

    @pl.when(has_next)
    def _():
        greet(2 * pair + 2)
        greet(2 * pair + 3)

    @pl.when(has_prev)
    def _():
        greet(2 * pair - 2)
        greet(2 * pair - 1)

    @pl.when(has_next2)
    def _():
        greet(2 * pair + 4)
        greet(2 * pair + 5)

    @pl.when(has_prev2)
    def _():
        greet(2 * pair - 3)

    for gl in range(2):
        for copy in own[gl]:
            copy.start()

    segw[3 + core] = jnp.broadcast_to(seg_in[...], (8, TOK))

    @pl.when(jnp.logical_not(has_prev2))
    def _():
        for gl in range(2):
            kw[gl, 0] = jnp.zeros((TOK, HEAD), jnp.bfloat16)
            vw[gl, 0] = jnp.zeros((TOK, HEAD), jnp.bfloat16)
        segw[0] = jnp.full((8, TOK), -1, jnp.int32)

    @pl.when(jnp.logical_not(has_prev))
    def _():
        for slot in (1, 2):
            for gl in range(2):
                kw[gl, slot] = jnp.zeros((TOK, HEAD), jnp.bfloat16)
                vw[gl, slot] = jnp.zeros((TOK, HEAD), jnp.bfloat16)
            segw[slot] = jnp.full((8, TOK), -1, jnp.int32)

    @pl.when(jnp.logical_not(has_next))
    def _():
        back[:, :, 0:2] = jnp.zeros((2, 2, 2, TOK, HEAD), jnp.bfloat16)

    @pl.when(jnp.logical_not(has_next2))
    def _():
        back[:, :, 2:4] = jnp.zeros((2, 2, 2, TOK, HEAD), jnp.bfloat16)

    signals = (
        1 + 2 * has_next.astype(jnp.int32) + 2 * has_prev.astype(jnp.int32)
        + 2 * has_next2.astype(jnp.int32) + has_prev2.astype(jnp.int32)
    )
    pl.semaphore_wait(barrier, signals)

    targets = [
        (0, 2 * pair + 2, has_next, 1 + core, 0),
        (1, 2 * pair + 3, has_next, 1 + core, 2),
        (2, 2 * pair + 4, has_next2, 0, 0),
        (3, 2 * pair + 5, has_next2, 0, 2),
        (4, partner, None, 3 + core, 2 * other),
    ]

    def guarded(cond, fn):
        if cond is None:
            fn()
        else:
            pl.when(cond)(fn)

    def seg_copy(target):
        n, p, _, slot, _ = target
        return pltpu.make_async_remote_copy(
            segw.at[3 + core], segw.at[slot], seg_send.at[n], seg_recv.at[slot], place(p), MESH
        )

    def kv_copies(target, gl):
        n, p, _, slot, head = target
        cols = kv_cols(head + gl)
        return (
            pltpu.make_async_remote_copy(
                k_in.at[:, cols], kw.at[gl, slot], kv_send.at[0, gl, n], kv_recv.at[0, gl, slot], place(p), MESH
            ),
            pltpu.make_async_remote_copy(
                v_in.at[:, cols], vw.at[gl, slot], kv_send.at[1, gl, n], kv_recv.at[1, gl, slot], place(p), MESH
            ),
        )

    def q_copies(gl):
        cols = q_cols(2 * other + gl)
        return (
            pltpu.make_async_remote_copy(
                q_in.at[:, cols], qb.at[gl, core], q_send.at[0, gl], q_recv.at[0, gl], place(partner), MESH
            ),
            pltpu.make_async_remote_copy(
                o_in.at[:, cols], ob.at[gl, core], q_send.at[1, gl], q_recv.at[1, gl], place(partner), MESH
            ),
        )

    for target in targets:
        def start_seg(target=target):
            seg_copy(target).start()
        guarded(target[2], start_seg)
    for gl in range(2):
        for target in targets:
            def start_kv(target=target, gl=gl):
                for copy in kv_copies(target, gl):
                    copy.start()
            guarded(target[2], start_kv)
        for copy in q_copies(gl):
            copy.start()

    def landed(ref, sem):
        pltpu.make_async_remote_copy(ref, ref, sem, sem, place(partner), MESH).wait_recv()

    def each_arrival(fn):
        guarded(has_prev2, lambda: fn(0))

        def near():
            fn(1)
            fn(2)
        guarded(has_prev, near)
        fn(3 + other)

    each_arrival(lambda slot: landed(segw.at[slot], seg_recv.at[slot]))
    row = lax.broadcasted_iota(jnp.int32, (TOK, TOK), 0)
    col = lax.broadcasted_iota(jnp.int32, (TOK, TOK), 1)
    key_seg = [
        jnp.broadcast_to(segw[slot, 0:1, :].astype(jnp.float32), (TOK, TOK)).T for slot in range(SLOTS)
    ]
    for t in range(2):
        query_seg = segw[3 + t, 0:1, :].astype(jnp.float32)
        for b in range(4):
            ok = key_seg[t + b] == query_seg
            if b == 0:
                ok = jnp.logical_and(ok, row > col)
            if b == 3:
                ok = jnp.logical_and(ok, row <= col)
            bias[t, b] = jnp.where(ok, 0.0, -1e30)

    def kv_wait(gl):
        own[gl][0].wait()
        own[gl][1].wait()

        def one(slot):
            landed(kw.at[gl, slot], kv_recv.at[0, gl, slot])
            landed(vw.at[gl, slot], kv_recv.at[1, gl, slot])
        each_arrival(one)

    def q_wait(gl):
        own[gl][2].wait()
        own[gl][3].wait()
        landed(qb.at[gl, other], q_recv.at[0, gl])
        landed(ob.at[gl, other], q_recv.at[1, gl])

    def stacked(block):
        heads = block.shape[1] // HEAD
        return jnp.concatenate([block[:, i * HEAD : (i + 1) * HEAD] for i in range(heads)], 0)

    def dq_copies(gl, t):
        cols = q_cols(2 * core + gl)
        return (
            pltpu.make_async_copy(dqs.at[gl, t], dq_out.at[:, cols], dq_sem.at[gl, 0]),
            pltpu.make_async_remote_copy(
                dqs.at[gl, t], dq_out.at[:, cols], dq_sem.at[gl, 1], dq_recv.at[gl], place(partner), MESH
            ),
        )

    def unit(gl, t, first):
        keys = kw[gl, t : t + 4].reshape(4 * TOK, HEAD)
        vals = vw[gl, t : t + 4].reshape(4 * TOK, HEAD)
        keys_t = keys.astype(jnp.float32).T.astype(jnp.bfloat16)

        def step(hp, carry):
            cols = pl.ds(pl.multiple_of(hp * 2 * HEAD, 2 * HEAD), 2 * HEAD)
            q = stacked(qb[gl, t, :, cols])
            o = stacked(ob[gl, t, :, cols])
            mask = bias[t].reshape(4 * TOK, TOK)
            mask = jnp.concatenate([mask, mask], 1)
            s = lax.dot_general(keys, q, NT, preferred_element_type=jnp.float32) * TO_EXP2 + mask
            dp = lax.dot_general(vals, o, NT, preferred_element_type=jnp.float32)
            top = jnp.max(s, axis=0, keepdims=True)
            w = jnp.exp2(s - top)
            r = 1.0 / jnp.sum(w, axis=0, keepdims=True)
            delta = jnp.sum(w * dp, axis=0, keepdims=True) * r
            probs = w * r
            ds = (probs * (dp - delta)).astype(jnp.bfloat16)
            pb[:, cols] = probs.astype(jnp.bfloat16)
            sb[:, cols] = ds
            dq = (jnp.dot(keys_t, ds, preferred_element_type=jnp.float32) * INV_ROOT).T
            dqs[gl, t, :, cols] = jnp.concatenate([dq[:TOK], dq[TOK:]], 1).astype(jnp.bfloat16)
            return carry

        lax.fori_loop(0, GROUP // 2, step, 0)

        def send_local():
            dq_copies(gl, t)[0].start()

        def send_remote():
            dq_copies(gl, t)[1].start()

        pl.when(core == t)(send_local)
        pl.when(core != t)(send_remote)
        dk = jnp.dot(sb[...], stacked(qb[gl, t]), preferred_element_type=jnp.float32) * INV_ROOT
        dv = jnp.dot(pb[...], stacked(ob[gl, t]), preferred_element_type=jnp.float32)
        dk = dk.reshape(4, TOK, HEAD)
        dv = dv.reshape(4, TOK, HEAD)
        for b in range(4):
            slot = t + b
            if first or slot == 0 or slot == 4:
                acc_k[gl, slot] = dk[b]
                acc_v[gl, slot] = dv[b]
            else:
                acc_k[gl, slot] += dk[b]
                acc_v[gl, slot] += dv[b]

    homes = [
        (0, 2 * pair - 3, has_prev2, 0, 2 + core),
        (1, 2 * pair - 2, has_prev, 1, core),
        (2, 2 * pair - 1, has_prev, 2, core),
        (3, partner, None, 3 + other, 4),
    ]

    def back_copies(home, gl):
        n, p, _, slot, spot = home
        return [
            pltpu.make_async_remote_copy(
                stage.at[i, gl, n], back.at[i, gl, spot], back_send.at[i, gl, n],
                back_recv.at[i, gl, spot], place(p), MESH,
            )
            for i in range(2)
        ]

    def send_back(gl, numbers):
        for n in numbers:
            home = homes[n]
            slot = home[3]
            stage[0, gl, n] = acc_k[gl, slot].astype(jnp.bfloat16)
            stage[1, gl, n] = acc_v[gl, slot].astype(jnp.bfloat16)

            def start(home=home):
                for copy in back_copies(home, gl):
                    copy.start()
            guarded(home[2], start)

    kv_wait(0)
    q_wait(0)
    unit(0, 1, True)
    unit(0, 0, False)
    send_back(0, (0, 1, 2, 3))
    kv_wait(1)
    q_wait(1)
    unit(1, 0, True)
    send_back(1, (0,))
    unit(1, 1, False)
    send_back(1, (1, 2, 3))

    for gl in range(2):
        def near(gl=gl):
            for i in range(2):
                for spot in (0, 1):
                    landed(back.at[i, gl, spot], back_recv.at[i, gl, spot])
        guarded(has_next, near)

        def far(gl=gl):
            for i in range(2):
                for spot in (2, 3):
                    landed(back.at[i, gl, spot], back_recv.at[i, gl, spot])
        guarded(has_next2, far)
        for i in range(2):
            landed(back.at[i, gl, 4], back_recv.at[i, gl, 4])
        for i, acc, out in ((0, acc_k, dk_out), (1, acc_v, dv_out)):
            mine = acc[gl, 3 + core]
            mine += back[i, gl, core].astype(jnp.float32)
            mine += back[i, gl, 2 + core].astype(jnp.float32)
            out[:, kv_cols(2 * core + gl)] = mine.astype(jnp.bfloat16)
            rest = back[i, gl, 4].astype(jnp.float32)
            rest += back[i, gl, other].astype(jnp.float32)
            rest += back[i, gl, 2 + other].astype(jnp.float32)
            out[:, kv_cols(2 * other + gl)] = rest.astype(jnp.bfloat16)

    for target in targets:
        def sent(target=target):
            seg_copy(target).wait_send()
            for gl in range(2):
                for copy in kv_copies(target, gl):
                    copy.wait_send()
        guarded(target[2], sent)
    for gl in range(2):
        for copy in q_copies(gl):
            copy.wait_send()
        for home in homes:
            def returned(home=home, gl=gl):
                for copy in back_copies(home, gl):
                    copy.wait_send()
            guarded(home[2], returned)
        dq_copies(gl, 0)[0].wait()
        dq_copies(gl, 0)[1].wait_send()
        landed(dq_out.at[:, q_cols(2 * other + gl)], dq_recv.at[gl])


def body(count, inner, query_rows, key_rows, value_matrix, out_grad, segments):
    bf16, f32 = jnp.bfloat16, jnp.float32
    dma = pltpu.SemaphoreType.DMA
    anywhere = pl.BlockSpec(memory_space=pl.ANY)
    vmem = pl.BlockSpec(memory_space=pltpu.VMEM)
    return pl.pallas_call(
        functools.partial(kernel, inner, count),
        out_shape=(
            jax.ShapeDtypeStruct(query_rows.shape, bf16),
            jax.ShapeDtypeStruct(key_rows.shape, bf16),
            jax.ShapeDtypeStruct(value_matrix.shape, bf16),
        ),
        in_specs=[anywhere] * 4 + [vmem],
        out_specs=(anywhere, vmem, vmem),
        scratch_shapes=[
            pltpu.VMEM((2, 2, TOK, WIDE), bf16),
            pltpu.VMEM((2, 2, TOK, WIDE), bf16),
            pltpu.VMEM((2, SLOTS, TOK, HEAD), bf16),
            pltpu.VMEM((2, SLOTS, TOK, HEAD), bf16),
            pltpu.VMEM((SLOTS, 8, TOK), jnp.int32),
            pltpu.VMEM((2, 4, TOK, TOK), f32),
            pltpu.VMEM((4 * TOK, WIDE), bf16),
            pltpu.VMEM((4 * TOK, WIDE), bf16),
            pltpu.VMEM((2, 2, TOK, WIDE), bf16),
            pltpu.VMEM((2, SLOTS, TOK, HEAD), f32),
            pltpu.VMEM((2, SLOTS, TOK, HEAD), f32),
            pltpu.VMEM((2, 2, 4, TOK, HEAD), bf16),
            pltpu.VMEM((2, 2, 5, TOK, HEAD), bf16),
            dma((4, 2)),
            dma((5,)),
            dma((SLOTS,)),
            dma((2, 2, 5)),
            dma((2, 2, SLOTS)),
            dma((2, 2)),
            dma((2, 2)),
            dma((2, 2)),
            dma((2,)),
            dma((2, 2, 4)),
            dma((2, 2, 5)),
        ],
        compiler_params=pltpu.CompilerParams(
            collective_id=0, has_side_effects=True, vmem_limit_bytes=40 * 1024 * 1024
        ),
        cost_estimate=pl.CostEstimate(flops=2_700_000_000, bytes_accessed=4_000_000, transcendentals=2_097_152),
    )(query_rows, key_rows, value_matrix, out_grad, segments.reshape(1, TOK))


def solution(mesh):
    count, inner = mesh.size, mesh.shape["fsdp"]
    rows = P(("ctx", "fsdp"), None)
    return jax.shard_map(
        functools.partial(body, count, inner),
        mesh=mesh,
        in_specs=(rows, rows, rows, rows, P(("ctx", "fsdp"))),
        out_specs=(rows, rows, rows),
        check_vma=False,
    )
```

time: 136 us -> 41.7 us (0.31)
  the two profiles are of different devices: /device:TPU:7 before, /device:TPU:11 now
where the time goes in v1:
time: 41.7 us; the launch traced here: 41.4 us
  Pallas kernels  33.6 us (81%)
  local copies, waits for them, and re-layouts  7.19 us (17%)
  between operations  0.65 us (2%)
    pallas_call x1, Pallas kernels, body(): pl.pallas_call(functools.partial(kernel, inner, count), out_shape=(jax.Sh...  33.6 us
    unnamed x13, local copies, waits for them, and re-layouts  7.19 us

profile of v1, /device:TPU:11, one launch (start us, length us, event | category | flops | bytes accessed | tf_op | source)
XLA Modules:
  0.0 41.4 jit_solution(2651266125374606043)
XLA Ops:
  0.6 0.0 copy-start.4
  0.6 0.6 %copy-done.4 = s32[128]{0:T(128)S(1)} copy-done((s32[128]{0:T(128)S(1)}, s32[128]{0:T(128)}, u32[]{:S(2)}) %copy-start.4) | copy-done | bytes 536
  1.3 0.0 copy-start
  1.3 1.2 %copy-done = bf16[128,4096]{1,0:T(8,128)(2,1)S(1)} copy-done((bf16[128,4096]{1,0:T(8,128)(2,1)S(1)}, bf16[128,4096]{1,0:T(8,128)(2,1)}, u32[]{:S(2)}) %copy-start) | copy-done | bytes 1048600
  2.5 0.0 copy-start.1
  2.5 1.2 %copy-done.1 = bf16[128,4096]{1,0:T(8,128)(2,1)S(1)} copy-done((bf16[128,4096]{1,0:T(8,128)(2,1)S(1)}, bf16[128,4096]{1,0:T(8,128)(2,1)}, u32[]{:S(2)}) %copy-start.1) | copy-done | bytes 1048600
  3.7 0.0 copy-start.2
  3.7 0.9 %copy-done.2 = bf16[128,512]{1,0:T(8,128)(2,1)S(1)} copy-done((bf16[128,512]{1,0:T(8,128)(2,1)S(1)}, bf16[128,512]{1,0:T(8,128)(2,1)}, u32[]{:S(2)}) %copy-start.2) | copy-done | bytes 131096
  4.6 0.0 copy-start.3
  4.6 0.9 %copy-done.3 = bf16[128,512]{1,0:T(8,128)(2,1)S(1)} copy-done((bf16[128,512]{1,0:T(8,128)(2,1)S(1)}, bf16[128,512]{1,0:T(8,128)(2,1)}, u32[]{:S(2)}) %copy-start.3) | copy-done | bytes 131096
  5.5 33.6 %shard_map.76 = (bf16[128,4096]{1,0:T(8,128)(2,1)S(1)}, bf16[128,512]{1,0:T(8,128)(2,1)S(1)}, bf16[128,512]{1,0:T(8,128)(2,1)S(1)}) custom-call(bf16[128,4096]{1,0:T(8,128)(2,1)S(1)} %copy-done, bf16[128,512]{1,0:T(8,128)(2,1)S(1)} %copy-done.2, bf16[128,512]{1,0:T(8,128)(2,1)S(1)} %copy-done.3, bf16[128,4096]{1,0:T(8,128)(2,1)S(1)} %copy-done.1, ...), custom_call_target="tpu_custom_call" | custom-call | flops 2700000000 | bytes 4000000 | tf_op jit(solution)/shard_map/pallas_call | solution.py:373
  39.2 1.0 %copy.11 = bf16[128,4096]{1,0:T(8,128)(2,1)} copy(bf16[128,4096]{1,0:T(8,128)(2,1)S(1)} %get-tuple-element.6) | data formatting | bytes 2097152
  40.1 0.7 %copy.12 = bf16[128,512]{1,0:T(8,128)(2,1)} copy(bf16[128,512]{1,0:T(8,128)(2,1)S(1)} %get-tuple-element.7) | data formatting | bytes 262144
  40.8 0.7 %copy.13 = bf16[128,512]{1,0:T(8,128)(2,1)} copy(bf16[128,512]{1,0:T(8,128)(2,1)S(1)} %get-tuple-element.8) | data formatting | bytes 262144
Async XLA Ops:
  0.6 0.7 %copy-start.4 = (s32[128]{0:T(128)S(1)}, s32[128]{0:T(128)}, u32[]{:S(2)}) copy-start(s32[128]{0:T(128)} %param.9) | copy-start | bytes 1540
  1.3 1.2 %copy-start = (bf16[128,4096]{1,0:T(8,128)(2,1)S(1)}, bf16[128,4096]{1,0:T(8,128)(2,1)}, u32[]{:S(2)}) copy-start(bf16[128,4096]{1,0:T(8,128)(2,1)} %q_in.1) | copy-start | bytes 3145732
  2.5 1.2 %copy-start.1 = (bf16[128,4096]{1,0:T(8,128)(2,1)S(1)}, bf16[128,4096]{1,0:T(8,128)(2,1)}, u32[]{:S(2)}) copy-start(bf16[128,4096]{1,0:T(8,128)(2,1)} %o_in.1) | copy-start | bytes 3145732
  3.7 0.9 %copy-start.2 = (bf16[128,512]{1,0:T(8,128)(2,1)S(1)}, bf16[128,512]{1,0:T(8,128)(2,1)}, u32[]{:S(2)}) copy-start(bf16[128,512]{1,0:T(8,128)(2,1)} %k_in.1) | copy-start | bytes 393220
  4.6 0.9 %copy-start.3 = (bf16[128,512]{1,0:T(8,128)(2,1)S(1)}, bf16[128,512]{1,0:T(8,128)(2,1)}, u32[]{:S(2)}) copy-start(bf16[128,512]{1,0:T(8,128)(2,1)} %v_in.1) | copy-start | bytes 393220

commit v2 on v1

--- a/solution.py
+++ b/solution.py
@@ -24,7 +24,7 @@
     q_in, k_in, v_in, o_in, seg_in,
     dq_out, dk_out, dv_out,
     qb, ob, kw, vw, segw, bias, pb, sb, dqs, acc_k, acc_v, stage, back,
-    local_sem, seg_send, seg_recv, kv_send, kv_recv, q_send, q_recv,
+    local_sem, seg_local, seg_send, seg_recv, kv_send, kv_recv, q_send, q_recv,
     dq_sem, dq_recv, back_send, back_recv,
 ):
     pos = lax.axis_index("ctx") * inner + lax.axis_index("fsdp")
@@ -89,14 +89,15 @@
         for copy in own[gl]:
             copy.start()
 
-    segw[3 + core] = jnp.broadcast_to(seg_in[...], (8, TOK))
+    own_seg = pltpu.make_async_copy(seg_in, segw.at[3 + core], seg_local)
+    own_seg.start()
 
     @pl.when(jnp.logical_not(has_prev2))
     def _():
         for gl in range(2):
             kw[gl, 0] = jnp.zeros((TOK, HEAD), jnp.bfloat16)
             vw[gl, 0] = jnp.zeros((TOK, HEAD), jnp.bfloat16)
-        segw[0] = jnp.full((8, TOK), -1, jnp.int32)
+        segw[0] = jnp.full((1, TOK), -1, jnp.int32)
 
     @pl.when(jnp.logical_not(has_prev))
     def _():
@@ -104,7 +105,7 @@
             for gl in range(2):
                 kw[gl, slot] = jnp.zeros((TOK, HEAD), jnp.bfloat16)
                 vw[gl, slot] = jnp.zeros((TOK, HEAD), jnp.bfloat16)
-            segw[slot] = jnp.full((8, TOK), -1, jnp.int32)
+            segw[slot] = jnp.full((1, TOK), -1, jnp.int32)
 
     @pl.when(jnp.logical_not(has_next))
     def _():
@@ -137,7 +138,7 @@
     def seg_copy(target):
         n, p, _, slot, _ = target
         return pltpu.make_async_remote_copy(
-            segw.at[3 + core], segw.at[slot], seg_send.at[n], seg_recv.at[slot], place(p), MESH
+            seg_in, segw.at[slot], seg_send.at[n], seg_recv.at[slot], place(p), MESH
         )
 
     def kv_copies(target, gl):
@@ -167,7 +168,7 @@
         def start_seg(target=target):
             seg_copy(target).start()
         guarded(target[2], start_seg)
-    for gl in range(2):
+    def send_operands(gl):
         for target in targets:
             def start_kv(target=target, gl=gl):
                 for copy in kv_copies(target, gl):
@@ -176,19 +177,24 @@
         for copy in q_copies(gl):
             copy.start()
 
+    send_operands(0)
+
     def landed(ref, sem):
         pltpu.make_async_remote_copy(ref, ref, sem, sem, place(partner), MESH).wait_recv()
 
-    def each_arrival(fn):
-        guarded(has_prev2, lambda: fn(0))
-
+    def near_arrivals(fn):
         def near():
             fn(1)
             fn(2)
         guarded(has_prev, near)
         fn(3 + other)
 
-    each_arrival(lambda slot: landed(segw.at[slot], seg_recv.at[slot]))
+    def far_arrival(fn):
+        guarded(has_prev2, lambda: fn(0))
+
+    own_seg.wait()
+    near_arrivals(lambda slot: landed(segw.at[slot], seg_recv.at[slot]))
+    far_arrival(lambda slot: landed(segw.at[slot], seg_recv.at[slot]))
     row = lax.broadcasted_iota(jnp.int32, (TOK, TOK), 0)
     col = lax.broadcasted_iota(jnp.int32, (TOK, TOK), 1)
     key_seg = [
@@ -204,14 +210,19 @@
                 ok = jnp.logical_and(ok, row <= col)
             bias[t, b] = jnp.where(ok, 0.0, -1e30)
 
-    def kv_wait(gl):
-        own[gl][0].wait()
-        own[gl][1].wait()
-
+    def kv_landed(gl):
         def one(slot):
             landed(kw.at[gl, slot], kv_recv.at[0, gl, slot])
             landed(vw.at[gl, slot], kv_recv.at[1, gl, slot])
-        each_arrival(one)
+        return one
+
+    def kv_wait_near(gl):
+        own[gl][0].wait()
+        own[gl][1].wait()
+        near_arrivals(kv_landed(gl))
+
+    def kv_wait_far(gl):
+        far_arrival(kv_landed(gl))
 
     def q_wait(gl):
         own[gl][2].wait()
@@ -223,26 +234,25 @@
         heads = block.shape[1] // HEAD
         return jnp.concatenate([block[:, i * HEAD : (i + 1) * HEAD] for i in range(heads)], 0)
 
-    def dq_copies(gl, t):
+    def dq_local(gl, t):
         cols = q_cols(2 * core + gl)
-        return (
-            pltpu.make_async_copy(dqs.at[gl, t], dq_out.at[:, cols], dq_sem.at[gl, 0]),
-            pltpu.make_async_remote_copy(
-                dqs.at[gl, t], dq_out.at[:, cols], dq_sem.at[gl, 1], dq_recv.at[gl], place(partner), MESH
-            ),
+        return pltpu.make_async_copy(dqs.at[gl, t], dq_out.at[:, cols], dq_sem.at[gl, 0])
+
+    def dq_remote(gl, t):
+        cols = q_cols(2 * core + gl)
+        return pltpu.make_async_remote_copy(
+            dqs.at[gl, t], dq_out.at[:, cols], dq_sem.at[gl, 1], dq_recv.at[gl], place(partner), MESH
         )
 
-    def unit(gl, t, first):
+    def probs_and_grads(gl, t):
         keys = kw[gl, t : t + 4].reshape(4 * TOK, HEAD)
         vals = vw[gl, t : t + 4].reshape(4 * TOK, HEAD)
-        keys_t = keys.astype(jnp.float32).T.astype(jnp.bfloat16)
-
-        def step(hp, carry):
-            cols = pl.ds(pl.multiple_of(hp * 2 * HEAD, 2 * HEAD), 2 * HEAD)
+        mask = bias[t].reshape(4 * TOK, TOK)
+        mask = jnp.concatenate([mask, mask], 1)
+        for hp in range(GROUP // 2):
+            cols = slice(hp * 2 * HEAD, (hp + 1) * 2 * HEAD)
             q = stacked(qb[gl, t, :, cols])
             o = stacked(ob[gl, t, :, cols])
-            mask = bias[t].reshape(4 * TOK, TOK)
-            mask = jnp.concatenate([mask, mask], 1)
             s = lax.dot_general(keys, q, NT, preferred_element_type=jnp.float32) * TO_EXP2 + mask
             dp = lax.dot_general(vals, o, NT, preferred_element_type=jnp.float32)
             top = jnp.max(s, axis=0, keepdims=True)
@@ -250,35 +260,33 @@
             r = 1.0 / jnp.sum(w, axis=0, keepdims=True)
             delta = jnp.sum(w * dp, axis=0, keepdims=True) * r
             probs = w * r
-            ds = (probs * (dp - delta)).astype(jnp.bfloat16)
             pb[:, cols] = probs.astype(jnp.bfloat16)
-            sb[:, cols] = ds
-            dq = (jnp.dot(keys_t, ds, preferred_element_type=jnp.float32) * INV_ROOT).T
+            sb[:, cols] = (probs * (dp - delta)).astype(jnp.bfloat16)
+
+    def query_grads(gl, t):
+        keys = kw[gl, t : t + 4].reshape(4 * TOK, HEAD)
+        keys_t = keys.astype(jnp.float32).T.astype(jnp.bfloat16)
+        for hp in range(GROUP // 2):
+            cols = slice(hp * 2 * HEAD, (hp + 1) * 2 * HEAD)
+            dq = (jnp.dot(keys_t, sb[:, cols], preferred_element_type=jnp.float32) * INV_ROOT).T
             dqs[gl, t, :, cols] = jnp.concatenate([dq[:TOK], dq[TOK:]], 1).astype(jnp.bfloat16)
-            return carry
-
-        lax.fori_loop(0, GROUP // 2, step, 0)
-
-        def send_local():
-            dq_copies(gl, t)[0].start()
-
-        def send_remote():
-            dq_copies(gl, t)[1].start()
-
-        pl.when(core == t)(send_local)
-        pl.when(core != t)(send_remote)
-        dk = jnp.dot(sb[...], stacked(qb[gl, t]), preferred_element_type=jnp.float32) * INV_ROOT
-        dv = jnp.dot(pb[...], stacked(ob[gl, t]), preferred_element_type=jnp.float32)
-        dk = dk.reshape(4, TOK, HEAD)
-        dv = dv.reshape(4, TOK, HEAD)
-        for b in range(4):
+        pl.when(core == t)(lambda: dq_local(gl, t).start())
+        pl.when(core != t)(lambda: dq_remote(gl, t).start())
+
+    def key_grads(gl, t, lower, upper, first):
+        rows = slice(lower * TOK, upper * TOK)
+        dk = jnp.dot(sb[rows], stacked(qb[gl, t]), preferred_element_type=jnp.float32) * INV_ROOT
+        dv = jnp.dot(pb[rows], stacked(ob[gl, t]), preferred_element_type=jnp.float32)
+        dk = dk.reshape(upper - lower, TOK, HEAD)
+        dv = dv.reshape(upper - lower, TOK, HEAD)
+        for b in range(lower, upper):
             slot = t + b
             if first or slot == 0 or slot == 4:
-                acc_k[gl, slot] = dk[b]
-                acc_v[gl, slot] = dv[b]
+                acc_k[gl, slot] = dk[b - lower]
+                acc_v[gl, slot] = dv[b - lower]
             else:
-                acc_k[gl, slot] += dk[b]
-                acc_v[gl, slot] += dv[b]
+                acc_k[gl, slot] += dk[b - lower]
+                acc_v[gl, slot] += dv[b - lower]
 
     homes = [
         (0, 2 * pair - 3, has_prev2, 0, 2 + core),
@@ -309,17 +317,30 @@
                     copy.start()
             guarded(home[2], start)
 
-    kv_wait(0)
+    kv_wait_near(0)
     q_wait(0)
-    unit(0, 1, True)
-    unit(0, 0, False)
+    send_operands(1)
+    probs_and_grads(0, 1)
+    query_grads(0, 1)
+    key_grads(0, 1, 0, 4, True)
+    kv_wait_far(0)
+    probs_and_grads(0, 0)
+    key_grads(0, 0, 0, 4, False)
     send_back(0, (0, 1, 2, 3))
-    kv_wait(1)
+    query_grads(0, 0)
+    kv_wait_near(1)
+    kv_wait_far(1)
     q_wait(1)
-    unit(1, 0, True)
+    probs_and_grads(1, 0)
+    key_grads(1, 0, 0, 4, True)
     send_back(1, (0,))
-    unit(1, 1, False)
-    send_back(1, (1, 2, 3))
+    query_grads(1, 0)
+    probs_and_grads(1, 1)
+    key_grads(1, 1, 0, 2, False)
+    send_back(1, (1, 2))
+    key_grads(1, 1, 2, 4, False)
+    send_back(1, (3,))
+    query_grads(1, 1)
 
     for gl in range(2):
         def near(gl=gl):
@@ -360,15 +381,15 @@
                 for copy in back_copies(home, gl):
                     copy.wait_send()
             guarded(home[2], returned)
-        dq_copies(gl, 0)[0].wait()
-        dq_copies(gl, 0)[1].wait_send()
+        dq_local(gl, 0).wait()
+        dq_remote(gl, 0).wait_send()
         landed(dq_out.at[:, q_cols(2 * other + gl)], dq_recv.at[gl])
 
 
 def body(count, inner, query_rows, key_rows, value_matrix, out_grad, segments):
     bf16, f32 = jnp.bfloat16, jnp.float32
     dma = pltpu.SemaphoreType.DMA
-    anywhere = pl.BlockSpec(memory_space=pl.ANY)
+    hbm = pl.BlockSpec(memory_space=pltpu.HBM)
     vmem = pl.BlockSpec(memory_space=pltpu.VMEM)
     return pl.pallas_call(
         functools.partial(kernel, inner, count),
@@ -377,14 +398,14 @@
             jax.ShapeDtypeStruct(key_rows.shape, bf16),
             jax.ShapeDtypeStruct(value_matrix.shape, bf16),
         ),
-        in_specs=[anywhere] * 4 + [vmem],
-        out_specs=(anywhere, vmem, vmem),
+        in_specs=[hbm] * 5,
+        out_specs=(hbm, vmem, vmem),
         scratch_shapes=[
             pltpu.VMEM((2, 2, TOK, WIDE), bf16),
             pltpu.VMEM((2, 2, TOK, WIDE), bf16),
             pltpu.VMEM((2, SLOTS, TOK, HEAD), bf16),
             pltpu.VMEM((2, SLOTS, TOK, HEAD), bf16),
-            pltpu.VMEM((SLOTS, 8, TOK), jnp.int32),
+            pltpu.VMEM((SLOTS, 1, TOK), jnp.int32),
             pltpu.VMEM((2, 4, TOK, TOK), f32),
             pltpu.VMEM((4 * TOK, WIDE), bf16),
             pltpu.VMEM((4 * TOK, WIDE), bf16),
@@ -394,6 +415,7 @@
             pltpu.VMEM((2, 2, 4, TOK, HEAD), bf16),
             pltpu.VMEM((2, 2, 5, TOK, HEAD), bf16),
             dma((4, 2)),
+            dma,
             dma((5,)),
             dma((SLOTS,)),
             dma((2, 2, 5)),
@@ -406,7 +428,7 @@
             dma((2, 2, 5)),
         ],
         compiler_params=pltpu.CompilerParams(
-            collective_id=0, has_side_effects=True, vmem_limit_bytes=40 * 1024 * 1024
+            collective_id=0, has_side_effects=True, vmem_limit_bytes=63 * 1024 * 1024
         ),
         cost_estimate=pl.CostEstimate(flops=2_700_000_000, bytes_accessed=4_000_000, transcendentals=2_097_152),
     )(query_rows, key_rows, value_matrix, out_grad, segments.reshape(1, TOK))

time: 41.7 us -> 30.7 us (0.74)
  the two profiles are of different devices: /device:TPU:11 before, /device:TPU:7 now
where the time goes in v2:
time: 30.7 us; the launch traced here: 30.5 us
  Pallas kernels  25.9 us (84%)
  local copies, waits for them, and re-layouts  3.93 us (13%)
  between operations  0.65 us (2%)
    pallas_call x1, Pallas kernels, body(): pl.pallas_call(functools.partial(kernel, inner, count), out_shape=(jax.Sh...  25.9 us
    unnamed x7, local copies, waits for them, and re-layouts  3.93 us

profile of v2, /device:TPU:7, one launch (start us, length us, event | category | flops | bytes accessed | tf_op | source)
XLA Modules:
  0.0 30.5 jit_solution(10316277348213809353)
XLA Ops:
  0.6 25.9 %shard_map.76 = (bf16[128,4096]{1,0:T(8,128)(2,1)}, bf16[128,512]{1,0:T(8,128)(2,1)}, bf16[128,512]{1,0:T(8,128)(2,1)}) custom-call(bf16[128,4096]{1,0:T(8,128)(2,1)} %q_in.1, bf16[128,512]{1,0:T(8,128)(2,1)} %k_in.1, bf16[128,512]{1,0:T(8,128)(2,1)} %v_in.1, bf16[128,4096]{1,0:T(8,128)(2,1)} %o_in.1, s32[1,128]{1,0:T(1,128)} %bitcast.1), custom_call_target="tpu_custom_call" | custom-call | flops 2700000000 | bytes 4000000 | tf_op jit(solution)/shard_map/pallas_call | solution.py:394
  26.6 0.0 copy-start.1
  26.6 2.3 %copy.11 = bf16[128,4096]{1,0:T(8,128)(2,1)} copy(bf16[128,4096]{1,0:T(8,128)(2,1)} %get-tuple-element.6) | data formatting | bytes 2097152
  28.9 0.0 copy-done.1
  28.9 0.0 copy-start
  28.9 0.7 %copy.12 = bf16[128,512]{1,0:T(8,128)(2,1)} copy(bf16[128,512]{1,0:T(8,128)(2,1)S(1)} %copy-done.1) | data formatting | bytes 262144
  29.6 0.3 copy-done
  29.9 0.7 %copy.13 = bf16[128,512]{1,0:T(8,128)(2,1)} copy(bf16[128,512]{1,0:T(8,128)(2,1)S(1)} %copy-done) | data formatting | bytes 262144
Async XLA Ops:
  26.6 2.3 %copy-start.1 = (bf16[128,512]{1,0:T(8,128)(2,1)S(1)}, bf16[128,512]{1,0:T(8,128)(2,1)}, u32[]{:S(2)}) copy-start(bf16[128,512]{1,0:T(8,128)(2,1)} %get-tuple-element.7) | copy-start | bytes 393220
  28.9 1.0 %copy-start = (bf16[128,512]{1,0:T(8,128)(2,1)S(1)}, bf16[128,512]{1,0:T(8,128)(2,1)}, u32[]{:S(2)}) copy-start(bf16[128,512]{1,0:T(8,128)(2,1)} %get-tuple-element.8) | copy-start | bytes 393220

commit v3 on v2

--- a/solution.py
+++ b/solution.py
@@ -23,7 +23,7 @@
     inner, count,
     q_in, k_in, v_in, o_in, seg_in,
     dq_out, dk_out, dv_out,
-    qb, ob, kw, vw, segw, bias, pb, sb, dqs, acc_k, acc_v, stage, back,
+    qb, ob, kw, vw, segw, bias, dqs, acc_k, acc_v, stage, back,
     local_sem, seg_local, seg_send, seg_recv, kv_send, kv_recv, q_send, q_recv,
     dq_sem, dq_recv, back_send, back_recv,
 ):
@@ -244,49 +244,69 @@
             dqs.at[gl, t], dq_out.at[:, cols], dq_sem.at[gl, 1], dq_recv.at[gl], place(partner), MESH
         )
 
-    def probs_and_grads(gl, t):
+    def unit(gl, t, first, after):
         keys = kw[gl, t : t + 4].reshape(4 * TOK, HEAD)
         vals = vw[gl, t : t + 4].reshape(4 * TOK, HEAD)
+        keys_t = keys.astype(jnp.float32).T.astype(jnp.bfloat16)
         mask = bias[t].reshape(4 * TOK, TOK)
         mask = jnp.concatenate([mask, mask], 1)
-        for hp in range(GROUP // 2):
-            cols = slice(hp * 2 * HEAD, (hp + 1) * 2 * HEAD)
-            q = stacked(qb[gl, t, :, cols])
-            o = stacked(ob[gl, t, :, cols])
+        pairs_of_heads = GROUP // 2
+
+        def columns(hp):
+            return slice(hp * 2 * HEAD, (hp + 1) * 2 * HEAD)
+
+        def front(hp):
+            q = stacked(qb[gl, t, :, columns(hp)])
+            o = stacked(ob[gl, t, :, columns(hp)])
             s = lax.dot_general(keys, q, NT, preferred_element_type=jnp.float32) * TO_EXP2 + mask
             dp = lax.dot_general(vals, o, NT, preferred_element_type=jnp.float32)
+            return s, dp
+
+        def middle(s, dp):
             top = jnp.max(s, axis=0, keepdims=True)
             w = jnp.exp2(s - top)
-            r = 1.0 / jnp.sum(w, axis=0, keepdims=True)
-            delta = jnp.sum(w * dp, axis=0, keepdims=True) * r
-            probs = w * r
-            pb[:, cols] = probs.astype(jnp.bfloat16)
-            sb[:, cols] = (probs * (dp - delta)).astype(jnp.bfloat16)
-
-    def query_grads(gl, t):
-        keys = kw[gl, t : t + 4].reshape(4 * TOK, HEAD)
-        keys_t = keys.astype(jnp.float32).T.astype(jnp.bfloat16)
-        for hp in range(GROUP // 2):
-            cols = slice(hp * 2 * HEAD, (hp + 1) * 2 * HEAD)
-            dq = (jnp.dot(keys_t, sb[:, cols], preferred_element_type=jnp.float32) * INV_ROOT).T
-            dqs[gl, t, :, cols] = jnp.concatenate([dq[:TOK], dq[TOK:]], 1).astype(jnp.bfloat16)
+            total = jnp.sum(w, axis=0, keepdims=True)
+            delta = jnp.sum(w * dp, axis=0, keepdims=True) / total
+            probs = jnp.exp2(s - (top + jnp.log2(total)))
+            return probs.astype(jnp.bfloat16), (probs * (dp - delta)).astype(jnp.bfloat16)
+
+        def rear(hp, probs, ds, sums):
+            q = stacked(qb[gl, t, :, columns(hp)])
+            o = stacked(ob[gl, t, :, columns(hp)])
+            dk = jnp.dot(ds, q, preferred_element_type=jnp.float32)
+            dv = jnp.dot(probs, o, preferred_element_type=jnp.float32)
+            if sums is not None:
+                dk, dv = sums[0] + dk, sums[1] + dv
+            return dk, dv
+
+        def query_side(hp, ds):
+            dq = (jnp.dot(keys_t, ds, preferred_element_type=jnp.float32) * INV_ROOT).T
+            dqs[gl, t, :, columns(hp)] = jnp.concatenate([dq[:TOK], dq[TOK:]], 1).astype(jnp.bfloat16)
+
+        ready = front(0)
+        sums, last = None, None
+        for hp in range(pairs_of_heads):
+            following = front(hp + 1) if hp + 1 < pairs_of_heads else None
+            now = middle(*ready)
+            if last is not None:
+                sums = rear(hp - 1, *last, sums)
+                query_side(hp - 1, last[1])
+            ready, last = following, now
+        dk, dv = rear(pairs_of_heads - 1, *last, sums)
+        dk = (dk * INV_ROOT).reshape(4, TOK, HEAD)
+        dv = dv.reshape(4, TOK, HEAD)
+        for b in range(4):
+            slot = t + b
+            if first or slot == 0 or slot == 4:
+                acc_k[gl, slot] = dk[b]
+                acc_v[gl, slot] = dv[b]
+            else:
+                acc_k[gl, slot] += dk[b]
+                acc_v[gl, slot] += dv[b]
+        query_side(pairs_of_heads - 1, last[1])
+        after()
         pl.when(core == t)(lambda: dq_local(gl, t).start())
         pl.when(core != t)(lambda: dq_remote(gl, t).start())
-
-    def key_grads(gl, t, lower, upper, first):
-        rows = slice(lower * TOK, upper * TOK)
-        dk = jnp.dot(sb[rows], stacked(qb[gl, t]), preferred_element_type=jnp.float32) * INV_ROOT
-        dv = jnp.dot(pb[rows], stacked(ob[gl, t]), preferred_element_type=jnp.float32)
-        dk = dk.reshape(upper - lower, TOK, HEAD)
-        dv = dv.reshape(upper - lower, TOK, HEAD)
-        for b in range(lower, upper):
-            slot = t + b
-            if first or slot == 0 or slot == 4:
-                acc_k[gl, slot] = dk[b - lower]
-                acc_v[gl, slot] = dv[b - lower]
-            else:
-                acc_k[gl, slot] += dk[b - lower]
-                acc_v[gl, slot] += dv[b - lower]
 
     homes = [
         (0, 2 * pair - 3, has_prev2, 0, 2 + core),
@@ -320,27 +340,14 @@
     kv_wait_near(0)
     q_wait(0)
     send_operands(1)
-    probs_and_grads(0, 1)
-    query_grads(0, 1)
-    key_grads(0, 1, 0, 4, True)
+    unit(0, 1, True, lambda: None)
     kv_wait_far(0)
-    probs_and_grads(0, 0)
-    key_grads(0, 0, 0, 4, False)
-    send_back(0, (0, 1, 2, 3))
-    query_grads(0, 0)
+    unit(0, 0, False, lambda: send_back(0, (0, 1, 2, 3)))
     kv_wait_near(1)
     kv_wait_far(1)
     q_wait(1)
-    probs_and_grads(1, 0)
-    key_grads(1, 0, 0, 4, True)
-    send_back(1, (0,))
-    query_grads(1, 0)
-    probs_and_grads(1, 1)
-    key_grads(1, 1, 0, 2, False)
-    send_back(1, (1, 2))
-    key_grads(1, 1, 2, 4, False)
-    send_back(1, (3,))
-    query_grads(1, 1)
+    unit(1, 0, True, lambda: send_back(1, (0,)))
+    unit(1, 1, False, lambda: send_back(1, (1, 2, 3)))
 
     for gl in range(2):
         def near(gl=gl):
@@ -386,12 +393,26 @@
         landed(dq_out.at[:, q_cols(2 * other + gl)], dq_recv.at[gl])
 
 
+def finish(dq, dk, dv, dq_out, dk_out, dv_out, sem):
+    rows = TOK // 4
+    copies = [
+        pltpu.make_async_copy(dq.at[i * rows : (i + 1) * rows], dq_out.at[i * rows : (i + 1) * rows], sem.at[i])
+        for i in range(4)
+    ]
+    copies.append(pltpu.make_async_copy(dk, dk_out, sem.at[4]))
+    copies.append(pltpu.make_async_copy(dv, dv_out, sem.at[5]))
+    for copy in copies:
+        copy.start()
+    for copy in copies:
+        copy.wait()
+
+
 def body(count, inner, query_rows, key_rows, value_matrix, out_grad, segments):
     bf16, f32 = jnp.bfloat16, jnp.float32
     dma = pltpu.SemaphoreType.DMA
     hbm = pl.BlockSpec(memory_space=pltpu.HBM)
     vmem = pl.BlockSpec(memory_space=pltpu.VMEM)
-    return pl.pallas_call(
+    parts = pl.pallas_call(
         functools.partial(kernel, inner, count),
         out_shape=(
             jax.ShapeDtypeStruct(query_rows.shape, bf16),
@@ -407,8 +428,6 @@
             pltpu.VMEM((2, SLOTS, TOK, HEAD), bf16),
             pltpu.VMEM((SLOTS, 1, TOK), jnp.int32),
             pltpu.VMEM((2, 4, TOK, TOK), f32),
-            pltpu.VMEM((4 * TOK, WIDE), bf16),
-            pltpu.VMEM((4 * TOK, WIDE), bf16),
             pltpu.VMEM((2, 2, TOK, WIDE), bf16),
             pltpu.VMEM((2, SLOTS, TOK, HEAD), f32),
             pltpu.VMEM((2, SLOTS, TOK, HEAD), f32),
@@ -432,6 +451,14 @@
         ),
         cost_estimate=pl.CostEstimate(flops=2_700_000_000, bytes_accessed=4_000_000, transcendentals=2_097_152),
     )(query_rows, key_rows, value_matrix, out_grad, segments.reshape(1, TOK))
+    return pl.pallas_call(
+        finish,
+        out_shape=tuple(jax.ShapeDtypeStruct(part.shape, bf16) for part in parts),
+        in_specs=[hbm] * 3,
+        out_specs=(hbm,) * 3,
+        scratch_shapes=[dma((6,))],
+        compiler_params=pltpu.CompilerParams(vmem_limit_bytes=63 * 1024 * 1024),
+    )(*parts)
 
 
 def solution(mesh):

time: 30.7 us -> 66.4 us (2.16)
  Pallas kernels: 25.9 us -> 65.7 us
  local copies, waits for them, and re-layouts: 3.93 us -> 0 us
    pallas_call x0 -> x1, Pallas kernels: none -> 40.9 us  [body(): pl.pallas_call(finish, out_shape=tuple((jax.ShapeDtypeStruct(part.shape,...]
    unnamed x7 -> x0, local copies, waits for them, and re-layouts: 3.93 us -> none
    pallas_call x1, Pallas kernels: 25.9 us -> 24.8 us  [body(): pl.pallas_call(functools.partial(kernel, inner, count), out_shape=(jax.Sh...]
where the time goes in v3:
time: 66.4 us; the launch traced here: 66.3 us
  Pallas kernels  65.7 us (99%)
    pallas_call x1, Pallas kernels, body(): pl.pallas_call(finish, out_shape=tuple((jax.ShapeDtypeStruct(part.shape,...  40.9 us
    pallas_call x1, Pallas kernels, body(): pl.pallas_call(functools.partial(kernel, inner, count), out_shape=(jax.Sh...  24.8 us

profile of v3, /device:TPU:7, one launch (start us, length us, event | category | flops | bytes accessed | tf_op | source)
XLA Modules:
  0.0 66.3 jit_solution(18388616893475357121)
XLA Ops:
  0.6 24.8 %shard_map.76 = (bf16[128,4096]{1,0:T(8,128)(2,1)}, bf16[128,512]{1,0:T(8,128)(2,1)}, bf16[128,512]{1,0:T(8,128)(2,1)}) custom-call(bf16[128,4096]{1,0:T(8,128)(2,1)} %q_in.1, bf16[128,512]{1,0:T(8,128)(2,1)} %k_in.1, bf16[128,512]{1,0:T(8,128)(2,1)} %v_in.1, bf16[128,4096]{1,0:T(8,128)(2,1)} %o_in.1, s32[1,128]{1,0:T(1,128)} %bitcast.1), custom_call_target="tpu_custom_call" | custom-call | flops 2700000000 | bytes 4000000 | tf_op jit(solution)/shard_map/pallas_call | solution.py:415
  25.4 40.9 %shard_map.77 = (bf16[128,4096]{1,0:T(8,128)(2,1)}, bf16[128,512]{1,0:T(8,128)(2,1)}, bf16[128,512]{1,0:T(8,128)(2,1)}) custom-call(bf16[128,4096]{1,0:T(8,128)(2,1)} %get-tuple-element.6.dq, bf16[128,512]{1,0:T(8,128)(2,1)} %get-tuple-element.7.dk, bf16[128,512]{1,0:T(8,128)(2,1)} %get-tuple-element.8.dv), custom_call_target="tpu_custom_call" | custom-call | tf_op jit(solution)/shard_map/pallas_call | solution.py:454

commit v4 on v3

--- a/solution.py
+++ b/solution.py
@@ -14,7 +14,6 @@
 SLOTS = 5
 WIDE = GROUP * HEAD
 INV_ROOT = 1.0 / math.sqrt(HEAD)
-TO_EXP2 = INV_ROOT * math.log2(math.e)
 MESH = pl.DeviceIdType.MESH
 NT = (((1,), (1,)), ((), ()))
 
@@ -168,16 +167,19 @@
         def start_seg(target=target):
             seg_copy(target).start()
         guarded(target[2], start_seg)
-    def send_operands(gl):
-        for target in targets:
+    def send_operands(gl, chosen):
+        for target in chosen:
             def start_kv(target=target, gl=gl):
                 for copy in kv_copies(target, gl):
                     copy.start()
             guarded(target[2], start_kv)
+
+    def send_queries(gl):
         for copy in q_copies(gl):
             copy.start()
 
-    send_operands(0)
+    send_operands(0, targets[:2] + targets[4:])
+    send_queries(0)
 
     def landed(ref, sem):
         pltpu.make_async_remote_copy(ref, ref, sem, sem, place(partner), MESH).wait_recv()
@@ -244,7 +246,7 @@
             dqs.at[gl, t], dq_out.at[:, cols], dq_sem.at[gl, 1], dq_recv.at[gl], place(partner), MESH
         )
 
-    def unit(gl, t, first, after):
+    def unit(gl, t, first, after, split=False):
         keys = kw[gl, t : t + 4].reshape(4 * TOK, HEAD)
         vals = vw[gl, t : t + 4].reshape(4 * TOK, HEAD)
         keys_t = keys.astype(jnp.float32).T.astype(jnp.bfloat16)
@@ -258,16 +260,16 @@
         def front(hp):
             q = stacked(qb[gl, t, :, columns(hp)])
             o = stacked(ob[gl, t, :, columns(hp)])
-            s = lax.dot_general(keys, q, NT, preferred_element_type=jnp.float32) * TO_EXP2 + mask
+            s = lax.dot_general(keys, q, NT, preferred_element_type=jnp.float32) * INV_ROOT + mask
             dp = lax.dot_general(vals, o, NT, preferred_element_type=jnp.float32)
             return s, dp
 
         def middle(s, dp):
             top = jnp.max(s, axis=0, keepdims=True)
-            w = jnp.exp2(s - top)
+            w = jnp.exp(s - top)
             total = jnp.sum(w, axis=0, keepdims=True)
             delta = jnp.sum(w * dp, axis=0, keepdims=True) / total
-            probs = jnp.exp2(s - (top + jnp.log2(total)))
+            probs = jnp.exp(s - (top + jnp.log(total)))
             return probs.astype(jnp.bfloat16), (probs * (dp - delta)).astype(jnp.bfloat16)
 
         def rear(hp, probs, ds, sums):
@@ -279,32 +281,50 @@
                 dk, dv = sums[0] + dk, sums[1] + dv
             return dk, dv
 
+        def settle(dk, dv, lower):
+            count = dk.shape[0] // TOK
+            dk = (dk * INV_ROOT).reshape(count, TOK, HEAD)
+            dv = dv.reshape(count, TOK, HEAD)
+            for b in range(count):
+                slot = t + lower + b
+                if first or slot == 0 or slot == 4:
+                    acc_k[gl, slot] = dk[b]
+                    acc_v[gl, slot] = dv[b]
+                else:
+                    acc_k[gl, slot] += dk[b]
+                    acc_v[gl, slot] += dv[b]
+
         def query_side(hp, ds):
             dq = (jnp.dot(keys_t, ds, preferred_element_type=jnp.float32) * INV_ROOT).T
             dqs[gl, t, :, columns(hp)] = jnp.concatenate([dq[:TOK], dq[TOK:]], 1).astype(jnp.bfloat16)
 
         ready = front(0)
-        sums, last = None, None
+        done = []
+        sums = None
         for hp in range(pairs_of_heads):
             following = front(hp + 1) if hp + 1 < pairs_of_heads else None
-            now = middle(*ready)
-            if last is not None:
-                sums = rear(hp - 1, *last, sums)
-                query_side(hp - 1, last[1])
-            ready, last = following, now
-        dk, dv = rear(pairs_of_heads - 1, *last, sums)
-        dk = (dk * INV_ROOT).reshape(4, TOK, HEAD)
-        dv = dv.reshape(4, TOK, HEAD)
-        for b in range(4):
-            slot = t + b
-            if first or slot == 0 or slot == 4:
-                acc_k[gl, slot] = dk[b]
-                acc_v[gl, slot] = dv[b]
-            else:
-                acc_k[gl, slot] += dk[b]
-                acc_v[gl, slot] += dv[b]
-        query_side(pairs_of_heads - 1, last[1])
-        after()
+            done.append(middle(*ready))
+            if hp > 0 and not split:
+                sums = rear(hp - 1, *done[hp - 1], sums)
+                query_side(hp - 1, done[hp - 1][1])
+            ready = following
+        if split:
+            probs = jnp.concatenate([d[0] for d in done], 1)
+            ds = jnp.concatenate([d[1] for d in done], 1)
+            q, o = stacked(qb[gl, t]), stacked(ob[gl, t])
+            for lower in (0, 2):
+                rows = slice(lower * TOK, (lower + 2) * TOK)
+                dk = jnp.dot(ds[rows], q, preferred_element_type=jnp.float32)
+                dv = jnp.dot(probs[rows], o, preferred_element_type=jnp.float32)
+                settle(dk, dv, lower)
+                after(lower)
+            for hp in range(pairs_of_heads):
+                query_side(hp, done[hp][1])
+        else:
+            sums = rear(pairs_of_heads - 1, *done[-1], sums)
+            settle(*sums, 0)
+            after(0)
+            query_side(pairs_of_heads - 1, done[-1][1])
         pl.when(core == t)(lambda: dq_local(gl, t).start())
         pl.when(core != t)(lambda: dq_remote(gl, t).start())
 
@@ -339,15 +359,17 @@
 
     kv_wait_near(0)
     q_wait(0)
-    send_operands(1)
-    unit(0, 1, True, lambda: None)
+    send_operands(0, targets[2:4])
+    send_operands(1, targets)
+    send_queries(1)
+    unit(0, 1, True, lambda lower: None)
     kv_wait_far(0)
-    unit(0, 0, False, lambda: send_back(0, (0, 1, 2, 3)))
+    unit(0, 0, False, lambda lower: send_back(0, (0, 1, 2, 3)))
     kv_wait_near(1)
     kv_wait_far(1)
     q_wait(1)
-    unit(1, 0, True, lambda: send_back(1, (0,)))
-    unit(1, 1, False, lambda: send_back(1, (1, 2, 3)))
+    unit(1, 0, True, lambda lower: send_back(1, (0,)))
+    unit(1, 1, False, lambda lower: send_back(1, (1, 2) if lower == 0 else (3,)), True)
 
     for gl in range(2):
         def near(gl=gl):
@@ -393,17 +415,22 @@
         landed(dq_out.at[:, q_cols(2 * other + gl)], dq_recv.at[gl])
 
 
-def finish(dq, dk, dv, dq_out, dk_out, dv_out, sem):
+def finish(dq, dk, dv, dq_out, dk_out, dv_out, dq_hold, kv_hold, in_sem, out_sem):
     rows = TOK // 4
-    copies = [
-        pltpu.make_async_copy(dq.at[i * rows : (i + 1) * rows], dq_out.at[i * rows : (i + 1) * rows], sem.at[i])
-        for i in range(4)
-    ]
-    copies.append(pltpu.make_async_copy(dk, dk_out, sem.at[4]))
-    copies.append(pltpu.make_async_copy(dv, dv_out, sem.at[5]))
-    for copy in copies:
+    trips = []
+    for i, (ref, out) in enumerate(((dk, dk_out), (dv, dv_out))):
+        trips.append((ref, kv_hold.at[i], out))
+    for i in range(4):
+        part = pl.ds(i * rows, rows)
+        trips.append((dq.at[part], dq_hold.at[part], dq_out.at[part]))
+    inward = [pltpu.make_async_copy(ref, hold, in_sem.at[i]) for i, (ref, hold, _) in enumerate(trips)]
+    outward = [pltpu.make_async_copy(hold, out, out_sem.at[i]) for i, (_, hold, out) in enumerate(trips)]
+    for copy in inward:
         copy.start()
-    for copy in copies:
+    for first, second in zip(inward, outward):
+        first.wait()
+        second.start()
+    for copy in outward:
         copy.wait()
 
 
@@ -456,7 +483,12 @@
         out_shape=tuple(jax.ShapeDtypeStruct(part.shape, bf16) for part in parts),
         in_specs=[hbm] * 3,
         out_specs=(hbm,) * 3,
-        scratch_shapes=[dma((6,))],
+        scratch_shapes=[
+            pltpu.VMEM(query_rows.shape, bf16),
+            pltpu.VMEM((2,) + key_rows.shape, bf16),
+            dma((6,)),
+            dma((6,)),
+        ],
         compiler_params=pltpu.CompilerParams(vmem_limit_bytes=63 * 1024 * 1024),
     )(*parts)
 

time: 66.4 us -> 29.3 us (0.44)
  the two profiles are of different devices: /device:TPU:7 before, /device:TPU:27 now
where the time goes in v4:
time: 29.3 us; the launch traced here: 29.2 us
  Pallas kernels  28.5 us (97%)
  between operations  0.64 us (2%)
    pallas_call x1, Pallas kernels, body(): pl.pallas_call(functools.partial(kernel, inner, count), out_shape=(jax.Sh...  26.4 us
    pallas_call x1, Pallas kernels, body(): pl.pallas_call(finish, out_shape=tuple((jax.ShapeDtypeStruct(part.shape,...  2.15 us

profile of v4, /device:TPU:27, one launch (start us, length us, event | category | flops | bytes accessed | tf_op | source)
XLA Modules:
  0.0 29.2 jit_solution(17098654336429402415)
XLA Ops:
  0.6 26.4 %shard_map.76 = (bf16[128,4096]{1,0:T(8,128)(2,1)}, bf16[128,512]{1,0:T(8,128)(2,1)}, bf16[128,512]{1,0:T(8,128)(2,1)}) custom-call(bf16[128,4096]{1,0:T(8,128)(2,1)} %q_in.1, bf16[128,512]{1,0:T(8,128)(2,1)} %k_in.1, bf16[128,512]{1,0:T(8,128)(2,1)} %v_in.1, bf16[128,4096]{1,0:T(8,128)(2,1)} %o_in.1, s32[1,128]{1,0:T(1,128)} %bitcast.1), custom_call_target="tpu_custom_call" | custom-call | flops 2700000000 | bytes 4000000 | tf_op jit(solution)/shard_map/pallas_call | solution.py:442
  27.0 2.1 %shard_map.77 = (bf16[128,4096]{1,0:T(8,128)(2,1)}, bf16[128,512]{1,0:T(8,128)(2,1)}, bf16[128,512]{1,0:T(8,128)(2,1)}) custom-call(bf16[128,4096]{1,0:T(8,128)(2,1)} %get-tuple-element.6.dq, bf16[128,512]{1,0:T(8,128)(2,1)} %get-tuple-element.7.dk, bf16[128,512]{1,0:T(8,128)(2,1)} %get-tuple-element.8.dv), custom_call_target="tpu_custom_call" | custom-call | tf_op jit(solution)/shard_map/pallas_call | solution.py:481

commit v5 on v4

v5 whole, which is shorter than its diff:
```python
import functools
import math

import jax
import jax.numpy as jnp
from jax import lax
from jax.experimental import pallas as pl
from jax.experimental.pallas import tpu as pltpu
from jax.sharding import PartitionSpec as P

HEAD = 128
GROUP = 8
TOK = 128
SLOTS = 5
WIDE = GROUP * HEAD
INV_ROOT = 1.0 / math.sqrt(HEAD)
MESH = pl.DeviceIdType.MESH
NT = (((1,), (1,)), ((), ()))


def kernel(
    inner, count,
    q_in, k_in, v_in, o_in, seg_in,
    dq_out, dk_out, dv_out,
    qb, ob, kv, segw, bias, dqs, acc, stage, back,
    local_sem, seg_send, seg_recv, near_send, near_recv, far_send, far_recv, side_send, side_recv,
    q_send, q_recv, dq_sem, dq_recv, back_send, back_recv,
):
    pos = lax.axis_index("ctx") * inner + lax.axis_index("fsdp")
    pairs = count // 2
    pair, core = pos // 2, pos % 2
    other = 1 - core

    def place(p):
        return (p // inner, p % inner)

    partner = 2 * pair + other
    has_next = pair + 1 < pairs
    has_next2 = jnp.logical_and(core == 1, pair + 2 < pairs)
    has_prev = pair >= 1
    has_prev2 = pair >= 2

    def kv_cols(h):
        return pl.ds(pl.multiple_of(h * HEAD, HEAD), HEAD)

    def q_cols(h):
        return pl.ds(pl.multiple_of(h * WIDE, WIDE), WIDE)

    def both_cols(p):
        return pl.ds(pl.multiple_of(p * 2 * HEAD, 2 * HEAD), 2 * HEAD)

    def wide_cols(p):
        return pl.ds(pl.multiple_of(p * 2 * WIDE, 2 * WIDE), 2 * WIDE)

    own = (
        pltpu.make_async_copy(k_in.at[:, both_cols(core)], kv.at[3 + core, 0], local_sem.at[0]),
        pltpu.make_async_copy(v_in.at[:, both_cols(core)], kv.at[3 + core, 1], local_sem.at[1]),
        pltpu.make_async_copy(q_in.at[:, wide_cols(core)], qb.at[core], local_sem.at[2]),
        pltpu.make_async_copy(o_in.at[:, wide_cols(core)], ob.at[core], local_sem.at[3]),
        pltpu.make_async_copy(seg_in, segw.at[3 + core], local_sem.at[4]),
    )

    barrier = pltpu.get_barrier_semaphore()

    def greet(p):
        pl.semaphore_signal(barrier, inc=1, device_id=place(p), device_id_type=MESH)

    greet(partner)

    @pl.when(has_next)
    def _():
        greet(2 * pair + 2)
        greet(2 * pair + 3)

    @pl.when(has_prev)
    def _():
        greet(2 * pair - 2)
        greet(2 * pair - 1)

    @pl.when(has_next2)
    def _():
        greet(2 * pair + 4)
        greet(2 * pair + 5)

    @pl.when(has_prev2)
    def _():
        greet(2 * pair - 3)

    for copy in own:
        copy.start()

    @pl.when(jnp.logical_not(has_prev2))
    def _():
        kv[0] = jnp.zeros((2, TOK, 2 * HEAD), jnp.bfloat16)
        segw[0] = jnp.full((1, TOK), -1, jnp.int32)

    @pl.when(jnp.logical_not(has_prev))
    def _():
        kv[1:3] = jnp.zeros((2, 2, TOK, 2 * HEAD), jnp.bfloat16)
        segw[1:3] = jnp.full((2, 1, TOK), -1, jnp.int32)

    @pl.when(jnp.logical_not(has_next))
    def _():
        back[:, 0:2] = jnp.zeros((2, 2, 2, TOK, HEAD), jnp.bfloat16)

    @pl.when(jnp.logical_not(has_next2))
    def _():
        back[:, 2:4] = jnp.zeros((2, 2, 2, TOK, HEAD), jnp.bfloat16)

    signals = (
        1 + 2 * has_next.astype(jnp.int32) + 2 * has_prev.astype(jnp.int32)
        + 2 * has_next2.astype(jnp.int32) + has_prev2.astype(jnp.int32)
    )
    pl.semaphore_wait(barrier, signals)

    def remote(src, dst, send, recv, p):
        return pltpu.make_async_remote_copy(src, dst, send, recv, place(p), MESH)

    def guarded(cond, fn):
        if cond is None:
            fn()
        else:
            pl.when(cond)(fn)

    targets = [
        (0, 2 * pair + 2, has_next, 1 + core, 0),
        (1, 2 * pair + 3, has_next, 1 + core, 1),
        (2, 2 * pair + 4, has_next2, 0, 0),
        (3, 2 * pair + 5, has_next2, 0, 1),
        (4, partner, None, 3 + core, other),
    ]

    def seg_copy(target):
        n, p, _, slot, _ = target
        return remote(seg_in, segw.at[slot], seg_send.at[n], seg_recv.at[slot], p)

    def send_near(gl):
        def start():
            for _, p, _, slot, two in targets[:2]:
                for i, ref in ((0, k_in), (1, v_in)):
                    remote(
                        ref.at[:, kv_cols(2 * two + gl)], kv.at[slot, i, :, gl * HEAD : (gl + 1) * HEAD],
                        near_send, near_recv.at[gl], p,
                    ).start()
        guarded(has_next, start)

    def send_far():
        def start():
            for _, p, _, slot, two in targets[2:4]:
                for i, ref in ((0, k_in), (1, v_in)):
                    remote(ref.at[:, both_cols(two)], kv.at[slot, i], far_send, far_recv, p).start()
        guarded(has_next2, start)

    def send_side():
        for i, ref in ((0, k_in), (1, v_in)):
            remote(ref.at[:, both_cols(other)], kv.at[3 + core, i], side_send, side_recv, partner).start()
        remote(q_in.at[:, wide_cols(other)], qb.at[core], q_send.at[0], q_recv.at[0], partner).start()
        remote(o_in.at[:, wide_cols(other)], ob.at[core], q_send.at[1], q_recv.at[1], partner).start()

    for target in targets:
        def start_seg(target=target):
            seg_copy(target).start()
        guarded(target[2], start_seg)
    send_near(0)
    send_side()

    def landed(ref, sem):
        remote(ref, ref, sem, sem, partner).wait_recv()

    def left(ref, sem):
        remote(ref, ref, sem, sem, partner).wait_send()

    def wait_near(gl):
        guarded(has_prev, lambda: landed(kv.at[1:3, :, :, gl * HEAD : (gl + 1) * HEAD], near_recv.at[gl]))

    def wait_far():
        guarded(has_prev2, lambda: landed(kv.at[0], far_recv))

    def wait_side():
        for copy in own[:4]:
            copy.wait()
        landed(kv.at[3 + other], side_recv)
        landed(qb.at[other], q_recv.at[0])
        landed(ob.at[other], q_recv.at[1])

    own[4].wait()
    landed(segw.at[3 + other], seg_recv.at[3 + other])

    def seg_near():
        landed(segw.at[1], seg_recv.at[1])
        landed(segw.at[2], seg_recv.at[2])
    guarded(has_prev, seg_near)
    guarded(has_prev2, lambda: landed(segw.at[0], seg_recv.at[0]))
    row = lax.broadcasted_iota(jnp.int32, (TOK, TOK), 0)
    col = lax.broadcasted_iota(jnp.int32, (TOK, TOK), 1)
    key_seg = [
        jnp.broadcast_to(segw[slot, 0:1, :].astype(jnp.float32), (TOK, TOK)).T for slot in range(SLOTS)
    ]
    for t in range(2):
        query_seg = segw[3 + t, 0:1, :].astype(jnp.float32)
        merged = jnp.where(row > col, key_seg[t], key_seg[t + 3])
        for b, seg in enumerate((merged, key_seg[t + 1], key_seg[t + 2])):
            bias[t, b] = jnp.where(seg == query_seg, 0.0, -1e30)

    def stacked(block):
        heads = block.shape[1] // HEAD
        return jnp.concatenate([block[:, i * HEAD : (i + 1) * HEAD] for i in range(heads)], 0)

    def dq_local(gl, t):
        cols = q_cols(2 * core + gl)
        return pltpu.make_async_copy(dqs.at[gl, t], dq_out.at[:, cols], dq_sem.at[gl, 0])

    def dq_remote(gl, t):
        cols = q_cols(2 * core + gl)
        return pltpu.make_async_remote_copy(
            dqs.at[gl, t], dq_out.at[:, cols], dq_sem.at[gl, 1], dq_recv.at[gl], place(partner), MESH
        )

    def unit(gl, t, first, after):
        lanes = slice(gl * HEAD, (gl + 1) * HEAD)
        keys = kv[t : t + 4, 0, :, lanes].reshape(4 * TOK, HEAD)
        vals = kv[t : t + 4, 1, :, lanes].reshape(4 * TOK, HEAD)
        keys_t = keys.astype(jnp.float32).T.astype(jnp.bfloat16)
        mask = bias[t].reshape(3 * TOK, TOK)
        mask = jnp.concatenate([mask, mask], 1)
        upper = jnp.concatenate([row > col, row > col], 1)
        kept = upper.astype(jnp.float32).astype(jnp.bfloat16)
        rest = jnp.logical_not(upper).astype(jnp.float32).astype(jnp.bfloat16)
        pairs_of_heads = GROUP // 2

        def columns(hp):
            return slice((gl * GROUP + hp * 2) * HEAD, (gl * GROUP + hp * 2 + 2) * HEAD)

        def merge(x):
            return jnp.concatenate([jnp.where(upper, x[:TOK], x[3 * TOK :]), x[TOK : 3 * TOK]], 0)

        def spread(x):
            return jnp.concatenate([x[:TOK] * kept, x[TOK:], x[:TOK] * rest], 0)

        def front(hp):
            q = stacked(qb[t, :, columns(hp)])
            o = stacked(ob[t, :, columns(hp)])
            s = merge(lax.dot_general(keys, q, NT, preferred_element_type=jnp.float32)) * INV_ROOT + mask
            dp = merge(lax.dot_general(vals, o, NT, preferred_element_type=jnp.float32))
            return s, dp

        def middle(s, dp):
            top = jnp.max(s, axis=0, keepdims=True)
            w = jnp.exp(s - top)
            total = jnp.sum(w, axis=0, keepdims=True)
            delta = jnp.sum(w * dp, axis=0, keepdims=True) / total
            probs = jnp.exp(s - (top + jnp.log(total)))
            ds = (probs * (dp - delta)).astype(jnp.bfloat16)
            return spread(probs.astype(jnp.bfloat16)), spread(ds)

        def rear(hp, probs, ds, sums):
            q = stacked(qb[t, :, columns(hp)])
            o = stacked(ob[t, :, columns(hp)])
            dk = jnp.dot(ds, q, preferred_element_type=jnp.float32)
            dv = jnp.dot(probs, o, preferred_element_type=jnp.float32)
            if sums is not None:
                dk, dv = sums[0] + dk, sums[1] + dv
            return dk, dv

        def query_side(hp, ds):
            dq = (jnp.dot(keys_t, ds, preferred_element_type=jnp.float32) * INV_ROOT).T
            dqs[gl, t, :, hp * 2 * HEAD : (hp + 1) * 2 * HEAD] = jnp.concatenate([dq[:TOK], dq[TOK:]], 1).astype(jnp.bfloat16)

        ready = front(0)
        done = []
        sums = None
        for hp in range(pairs_of_heads):
            following = front(hp + 1) if hp + 1 < pairs_of_heads else None
            done.append(middle(*ready))
            if hp > 0:
                sums = rear(hp - 1, *done[hp - 1], sums)
                query_side(hp - 1, done[hp - 1][1])
            ready = following
        dk, dv = rear(pairs_of_heads - 1, *done[-1], sums)
        dk = (dk * INV_ROOT).reshape(4, TOK, HEAD)
        dv = dv.reshape(4, TOK, HEAD)
        for b in range(4):
            slot = t + b
            if first or slot == 0 or slot == 4:
                acc[gl, slot, 0] = dk[b]
                acc[gl, slot, 1] = dv[b]
            else:
                acc[gl, slot, 0] += dk[b]
                acc[gl, slot, 1] += dv[b]
        after()
        query_side(pairs_of_heads - 1, done[-1][1])
        pl.when(core == t)(lambda: dq_local(gl, t).start())
        pl.when(core != t)(lambda: dq_remote(gl, t).start())

    homes = [
        (0, 2 * pair - 3, has_prev2, 0, 2 + core),
        (1, 2 * pair - 2, has_prev, 1, core),
        (2, 2 * pair - 1, has_prev, 2, core),
        (3, partner, None, 3 + other, 4),
    ]

    def back_copy(home, gl):
        n, p, _, slot, spot = home
        return remote(stage.at[gl, n], back.at[gl, spot], back_send.at[gl, n], back_recv.at[gl, spot // 2], p)

    def send_back(gl, numbers):
        for n in numbers:
            home = homes[n]
            stage[gl, n] = acc[gl, home[3]].astype(jnp.bfloat16)
        for n in numbers:
            home = homes[n]

            def start(home=home):
                back_copy(home, gl).start()
            guarded(home[2], start)

    wait_side()
    wait_near(0)
    send_far()
    send_near(1)
    unit(0, 1, True, lambda: None)
    wait_far()
    unit(0, 0, False, lambda: send_back(0, (0, 1, 2, 3)))
    wait_near(1)
    unit(1, 0, True, lambda: send_back(1, (0,)))
    unit(1, 1, False, lambda: send_back(1, (1, 2, 3)))

    for target in targets:
        def sent(target=target):
            seg_copy(target).wait_send()
        guarded(target[2], sent)
    guarded(has_next, lambda: left(kv.at[0:2], near_send))
    guarded(has_next2, lambda: left(kv.at[0:2], far_send))
    left(kv.at[0], side_send)
    left(qb.at[0], q_send.at[0])
    left(ob.at[0], q_send.at[1])
    dq_local(0, 0).wait()
    dq_local(1, 0).wait()

    for gl in range(2):
        def near(gl=gl):
            landed(back.at[gl, 0:2], back_recv.at[gl, 0])
        guarded(has_next, near)

        def far(gl=gl):
            landed(back.at[gl, 2:4], back_recv.at[gl, 1])
        guarded(has_next2, far)
        landed(back.at[gl, 4], back_recv.at[gl, 2])
        for i, out in ((0, dk_out), (1, dv_out)):
            mine = acc[gl, 3 + core, i]
            mine += back[gl, core, i].astype(jnp.float32)
            mine += back[gl, 2 + core, i].astype(jnp.float32)
            out[:, kv_cols(2 * core + gl)] = mine.astype(jnp.bfloat16)
            theirs = back[gl, 4, i].astype(jnp.float32)
            theirs += back[gl, other, i].astype(jnp.float32)
            theirs += back[gl, 2 + other, i].astype(jnp.float32)
            out[:, kv_cols(2 * other + gl)] = theirs.astype(jnp.bfloat16)

    for gl in range(2):
        for home in homes:
            def returned(home=home, gl=gl):
                back_copy(home, gl).wait_send()
            guarded(home[2], returned)
        dq_remote(gl, 0).wait_send()
        landed(dq_out.at[:, q_cols(2 * other + gl)], dq_recv.at[gl])


def finish(dq, dk, dv, dq_out, dk_out, dv_out, dq_hold, kv_hold, in_sem, out_sem):
    rows = TOK // 4
    trips = []
    for i, (ref, out) in enumerate(((dk, dk_out), (dv, dv_out))):
        trips.append((ref, kv_hold.at[i], out))
    for i in range(4):
        part = pl.ds(i * rows, rows)
        trips.append((dq.at[part], dq_hold.at[part], dq_out.at[part]))
    inward = [pltpu.make_async_copy(ref, hold, in_sem.at[i]) for i, (ref, hold, _) in enumerate(trips)]
    outward = [pltpu.make_async_copy(hold, out, out_sem.at[i]) for i, (_, hold, out) in enumerate(trips)]
    for copy in inward:
        copy.start()
    for first, second in zip(inward, outward):
        first.wait()
        second.start()
    for copy in outward:
        copy.wait()


def body(count, inner, query_rows, key_rows, value_matrix, out_grad, segments):
    bf16, f32 = jnp.bfloat16, jnp.float32
    dma = pltpu.SemaphoreType.DMA
    hbm = pl.BlockSpec(memory_space=pltpu.HBM)
    vmem = pl.BlockSpec(memory_space=pltpu.VMEM)
    parts = pl.pallas_call(
        functools.partial(kernel, inner, count),
        out_shape=(
            jax.ShapeDtypeStruct(query_rows.shape, bf16),
            jax.ShapeDtypeStruct(key_rows.shape, bf16),
            jax.ShapeDtypeStruct(value_matrix.shape, bf16),
        ),
        in_specs=[hbm] * 5,
        out_specs=(hbm, vmem, vmem),
        scratch_shapes=[
            pltpu.VMEM((2, TOK, 2 * WIDE), bf16),
            pltpu.VMEM((2, TOK, 2 * WIDE), bf16),
            pltpu.VMEM((SLOTS, 2, TOK, 2 * HEAD), bf16),
            pltpu.VMEM((SLOTS, 1, TOK), jnp.int32),
            pltpu.VMEM((2, 3, TOK, TOK), f32),
            pltpu.VMEM((2, 2, TOK, WIDE), bf16),
            pltpu.VMEM((2, SLOTS, 2, TOK, HEAD), f32),
            pltpu.VMEM((2, 4, 2, TOK, HEAD), bf16),
            pltpu.VMEM((2, 5, 2, TOK, HEAD), bf16),
            dma((5,)),
            dma((5,)),
            dma((SLOTS,)),
            dma,
            dma((2,)),
            dma,
            dma,
            dma,
            dma,
            dma((2,)),
            dma((2,)),
            dma((2, 2)),
            dma((2,)),
            dma((2, 4)),
            dma((2, 3)),
        ],
        compiler_params=pltpu.CompilerParams(
            collective_id=0, has_side_effects=True, vmem_limit_bytes=63 * 1024 * 1024
        ),
        cost_estimate=pl.CostEstimate(flops=2_700_000_000, bytes_accessed=4_000_000, transcendentals=2_097_152),
    )(query_rows, key_rows, value_matrix, out_grad, segments.reshape(1, TOK))
    return pl.pallas_call(
        finish,
        out_shape=tuple(jax.ShapeDtypeStruct(part.shape, bf16) for part in parts),
        in_specs=[hbm] * 3,
        out_specs=(hbm,) * 3,
        scratch_shapes=[
            pltpu.VMEM(query_rows.shape, bf16),
            pltpu.VMEM((2,) + key_rows.shape, bf16),
            dma((6,)),
            dma((6,)),
        ],
        compiler_params=pltpu.CompilerParams(vmem_limit_bytes=63 * 1024 * 1024),
    )(*parts)


def solution(mesh):
    count, inner = mesh.size, mesh.shape["fsdp"]
    rows = P(("ctx", "fsdp"), None)
    return jax.shard_map(
        functools.partial(body, count, inner),
        mesh=mesh,
        in_specs=(rows, rows, rows, rows, P(("ctx", "fsdp"))),
        out_specs=(rows, rows, rows),
        check_vma=False,
    )
```

time: 29.3 us -> 29 us (0.990)
  the two profiles are of different devices: /device:TPU:27 before, /device:TPU:7 now
where the time goes in v5:
time: 29 us; the launch traced here: 28.9 us
  Pallas kernels  28.2 us (97%)
  between operations  0.64 us (2%)
    pallas_call x1, Pallas kernels, body(): pl.pallas_call(functools.partial(kernel, inner, count), out_shape=(jax.Sh...  26.1 us
    pallas_call x1, Pallas kernels, body(): pl.pallas_call(finish, out_shape=tuple((jax.ShapeDtypeStruct(part.shape,...  2.15 us

profile of v5, /device:TPU:7, one launch (start us, length us, event | category | flops | bytes accessed | tf_op | source)
XLA Modules:
  0.0 28.9 jit_solution(10652400361428014638)
XLA Ops:
  0.6 26.1 %shard_map.76 = (bf16[128,4096]{1,0:T(8,128)(2,1)}, bf16[128,512]{1,0:T(8,128)(2,1)}, bf16[128,512]{1,0:T(8,128)(2,1)}) custom-call(bf16[128,4096]{1,0:T(8,128)(2,1)} %q_in.1, bf16[128,512]{1,0:T(8,128)(2,1)} %k_in.1, bf16[128,512]{1,0:T(8,128)(2,1)} %v_in.1, bf16[128,4096]{1,0:T(8,128)(2,1)} %o_in.1, s32[1,128]{1,0:T(1,128)} %bitcast.1), custom_call_target="tpu_custom_call" | custom-call | flops 2700000000 | bytes 4000000 | tf_op jit(solution)/shard_map/pallas_call | solution.py:392
  26.7 2.1 %shard_map.77 = (bf16[128,4096]{1,0:T(8,128)(2,1)}, bf16[128,512]{1,0:T(8,128)(2,1)}, bf16[128,512]{1,0:T(8,128)(2,1)}) custom-call(bf16[128,4096]{1,0:T(8,128)(2,1)} %get-tuple-element.6.dq, bf16[128,512]{1,0:T(8,128)(2,1)} %get-tuple-element.7.dk, bf16[128,512]{1,0:T(8,128)(2,1)} %get-tuple-element.8.dv), custom_call_target="tpu_custom_call" | custom-call | tf_op jit(solution)/shard_map/pallas_call | solution.py:432

commit v6 on v5

--- a/solution.py
+++ b/solution.py
@@ -216,7 +216,7 @@
             dqs.at[gl, t], dq_out.at[:, cols], dq_sem.at[gl, 1], dq_recv.at[gl], place(partner), MESH
         )
 
-    def unit(gl, t, first, after):
+    def unit(gl, t, first, after, last=None):
         lanes = slice(gl * HEAD, (gl + 1) * HEAD)
         keys = kv[t : t + 4, 0, :, lanes].reshape(4 * TOK, HEAD)
         vals = kv[t : t + 4, 1, :, lanes].reshape(4 * TOK, HEAD)
@@ -247,21 +247,34 @@
         def middle(s, dp):
             top = jnp.max(s, axis=0, keepdims=True)
             w = jnp.exp(s - top)
-            total = jnp.sum(w, axis=0, keepdims=True)
-            delta = jnp.sum(w * dp, axis=0, keepdims=True) / total
-            probs = jnp.exp(s - (top + jnp.log(total)))
+            scale = 1.0 / jnp.sum(w, axis=0, keepdims=True)
+            delta = jnp.sum(w * dp, axis=0, keepdims=True) * scale
+            probs = w * scale
             ds = (probs * (dp - delta)).astype(jnp.bfloat16)
             return spread(probs.astype(jnp.bfloat16)), spread(ds)
 
-        def rear(hp, probs, ds, sums):
+        def rear(hp, probs, ds, sums, rows):
             q = stacked(qb[t, :, columns(hp)])
             o = stacked(ob[t, :, columns(hp)])
-            dk = jnp.dot(ds, q, preferred_element_type=jnp.float32)
-            dv = jnp.dot(probs, o, preferred_element_type=jnp.float32)
+            dk = jnp.dot(ds[rows], q, preferred_element_type=jnp.float32)
+            dv = jnp.dot(probs[rows], o, preferred_element_type=jnp.float32)
             if sums is not None:
                 dk, dv = sums[0] + dk, sums[1] + dv
             return dk, dv
 
+        def settle(sums, lower):
+            count = sums[0].shape[0] // TOK
+            dk = (sums[0] * INV_ROOT).reshape(count, TOK, HEAD)
+            dv = sums[1].reshape(count, TOK, HEAD)
+            for b in range(count):
+                slot = t + lower + b
+                if first or slot == 0 or slot == 4:
+                    acc[gl, slot, 0] = dk[b]
+                    acc[gl, slot, 1] = dv[b]
+                else:
+                    acc[gl, slot, 0] += dk[b]
+                    acc[gl, slot, 1] += dv[b]
+
         def query_side(hp, ds):
             dq = (jnp.dot(keys_t, ds, preferred_element_type=jnp.float32) * INV_ROOT).T
             dqs[gl, t, :, hp * 2 * HEAD : (hp + 1) * 2 * HEAD] = jnp.concatenate([dq[:TOK], dq[TOK:]], 1).astype(jnp.bfloat16)
@@ -269,26 +282,29 @@
         ready = front(0)
         done = []
         sums = None
+        split = last is not None
+        early = slice(0, 2 * TOK) if split else slice(0, 4 * TOK)
+        late = slice(2 * TOK, 4 * TOK)
         for hp in range(pairs_of_heads):
             following = front(hp + 1) if hp + 1 < pairs_of_heads else None
             done.append(middle(*ready))
             if hp > 0:
-                sums = rear(hp - 1, *done[hp - 1], sums)
-                query_side(hp - 1, done[hp - 1][1])
+                sums = rear(hp - 1, *done[hp - 1], sums, early)
+                if not split:
+                    query_side(hp - 1, done[hp - 1][1])
             ready = following
-        dk, dv = rear(pairs_of_heads - 1, *done[-1], sums)
-        dk = (dk * INV_ROOT).reshape(4, TOK, HEAD)
-        dv = dv.reshape(4, TOK, HEAD)
-        for b in range(4):
-            slot = t + b
-            if first or slot == 0 or slot == 4:
-                acc[gl, slot, 0] = dk[b]
-                acc[gl, slot, 1] = dv[b]
-            else:
-                acc[gl, slot, 0] += dk[b]
-                acc[gl, slot, 1] += dv[b]
+        sums = rear(pairs_of_heads - 1, *done[-1], sums, early)
+        settle(sums, 0)
         after()
-        query_side(pairs_of_heads - 1, done[-1][1])
+        if split:
+            sums = None
+            for hp in range(pairs_of_heads):
+                sums = rear(hp, *done[hp], sums, late)
+                query_side(hp, done[hp][1])
+            settle(sums, 2)
+            last()
+        else:
+            query_side(pairs_of_heads - 1, done[-1][1])
         pl.when(core == t)(lambda: dq_local(gl, t).start())
         pl.when(core != t)(lambda: dq_remote(gl, t).start())
 
@@ -323,7 +339,7 @@
     unit(0, 0, False, lambda: send_back(0, (0, 1, 2, 3)))
     wait_near(1)
     unit(1, 0, True, lambda: send_back(1, (0,)))
-    unit(1, 1, False, lambda: send_back(1, (1, 2, 3)))
+    unit(1, 1, False, lambda: send_back(1, (1, 2)), lambda: send_back(1, (3,)))
 
     for target in targets:
         def sent(target=target):

time: 29 us -> 28.9 us (level)
  no operation moved by 1% of the time
where the time goes in v6:
time: 28.9 us; the launch traced here: 28.7 us
  Pallas kernels  28.1 us (97%)
  between operations  0.64 us (2%)
    pallas_call x1, Pallas kernels, body(): pl.pallas_call(functools.partial(kernel, inner, count), out_shape=(jax.Sh...  25.9 us
    pallas_call x1, Pallas kernels, body(): pl.pallas_call(finish, out_shape=tuple((jax.ShapeDtypeStruct(part.shape,...  2.15 us

profile of v6, /device:TPU:7, one launch (start us, length us, event | category | flops | bytes accessed | tf_op | source)
XLA Modules:
  0.0 28.7 jit_solution(15848044069487578790)
XLA Ops:
  0.6 25.9 %shard_map.76 = (bf16[128,4096]{1,0:T(8,128)(2,1)}, bf16[128,512]{1,0:T(8,128)(2,1)}, bf16[128,512]{1,0:T(8,128)(2,1)}) custom-call(bf16[128,4096]{1,0:T(8,128)(2,1)} %q_in.1, bf16[128,512]{1,0:T(8,128)(2,1)} %k_in.1, bf16[128,512]{1,0:T(8,128)(2,1)} %v_in.1, bf16[128,4096]{1,0:T(8,128)(2,1)} %o_in.1, s32[1,128]{1,0:T(1,128)} %bitcast.1), custom_call_target="tpu_custom_call" | custom-call | flops 2700000000 | bytes 4000000 | tf_op jit(solution)/shard_map/pallas_call | solution.py:408
  26.6 2.1 %shard_map.77 = (bf16[128,4096]{1,0:T(8,128)(2,1)}, bf16[128,512]{1,0:T(8,128)(2,1)}, bf16[128,512]{1,0:T(8,128)(2,1)}) custom-call(bf16[128,4096]{1,0:T(8,128)(2,1)} %get-tuple-element.6.dq, bf16[128,512]{1,0:T(8,128)(2,1)} %get-tuple-element.7.dk, bf16[128,512]{1,0:T(8,128)(2,1)} %get-tuple-element.8.dv), custom_call_target="tpu_custom_call" | custom-call | tf_op jit(solution)/shard_map/pallas_call | solution.py:448

commit v7 on v6

--- a/solution.py
+++ b/solution.py
@@ -144,11 +144,14 @@
                     ).start()
         guarded(has_next, start)
 
-    def send_far():
+    def send_far(gl):
         def start():
             for _, p, _, slot, two in targets[2:4]:
                 for i, ref in ((0, k_in), (1, v_in)):
-                    remote(ref.at[:, both_cols(two)], kv.at[slot, i], far_send, far_recv, p).start()
+                    remote(
+                        ref.at[:, kv_cols(2 * two + gl)], kv.at[slot, i, :, gl * HEAD : (gl + 1) * HEAD],
+                        far_send, far_recv.at[gl], p,
+                    ).start()
         guarded(has_next2, start)
 
     def send_side():
@@ -157,11 +160,11 @@
         remote(q_in.at[:, wide_cols(other)], qb.at[core], q_send.at[0], q_recv.at[0], partner).start()
         remote(o_in.at[:, wide_cols(other)], ob.at[core], q_send.at[1], q_recv.at[1], partner).start()
 
+    send_near(0)
     for target in targets:
         def start_seg(target=target):
             seg_copy(target).start()
         guarded(target[2], start_seg)
-    send_near(0)
     send_side()
 
     def landed(ref, sem):
@@ -173,8 +176,8 @@
     def wait_near(gl):
         guarded(has_prev, lambda: landed(kv.at[1:3, :, :, gl * HEAD : (gl + 1) * HEAD], near_recv.at[gl]))
 
-    def wait_far():
-        guarded(has_prev2, lambda: landed(kv.at[0], far_recv))
+    def wait_far(gl):
+        guarded(has_prev2, lambda: landed(kv.at[0, :, :, gl * HEAD : (gl + 1) * HEAD], far_recv.at[gl]))
 
     def wait_side():
         for copy in own[:4]:
@@ -332,12 +335,14 @@
 
     wait_side()
     wait_near(0)
-    send_far()
+    send_far(0)
     send_near(1)
     unit(0, 1, True, lambda: None)
-    wait_far()
+    send_far(1)
+    wait_far(0)
     unit(0, 0, False, lambda: send_back(0, (0, 1, 2, 3)))
     wait_near(1)
+    wait_far(1)
     unit(1, 0, True, lambda: send_back(1, (0,)))
     unit(1, 1, False, lambda: send_back(1, (1, 2)), lambda: send_back(1, (3,)))
 
@@ -430,7 +435,7 @@
             dma,
             dma((2,)),
             dma,
-            dma,
+            dma((2,)),
             dma,
             dma,
             dma((2,)),

time: 28.9 us -> 27.9 us (0.965)
  Pallas kernels: 28.1 us -> 26.9 us
    pallas_call x1, Pallas kernels: 25.9 us -> 24.7 us  [body(): pl.pallas_call(functools.partial(kernel, inner, count), out_shape=(jax.Sh...]
where the time goes in v7:
time: 27.9 us; the launch traced here: 27.5 us
  Pallas kernels  26.9 us (96%)
  between operations  0.64 us (2%)
    pallas_call x1, Pallas kernels, body(): pl.pallas_call(functools.partial(kernel, inner, count), out_shape=(jax.Sh...  24.7 us
    pallas_call x1, Pallas kernels, body(): pl.pallas_call(finish, out_shape=tuple((jax.ShapeDtypeStruct(part.shape,...  2.15 us

profile of v7, /device:TPU:7, one launch (start us, length us, event | category | flops | bytes accessed | tf_op | source)
XLA Modules:
  0.0 27.5 jit_solution(1917414693295543753)
XLA Ops:
  0.6 24.7 %shard_map.76 = (bf16[128,4096]{1,0:T(8,128)(2,1)}, bf16[128,512]{1,0:T(8,128)(2,1)}, bf16[128,512]{1,0:T(8,128)(2,1)}) custom-call(bf16[128,4096]{1,0:T(8,128)(2,1)} %q_in.1, bf16[128,512]{1,0:T(8,128)(2,1)} %k_in.1, bf16[128,512]{1,0:T(8,128)(2,1)} %v_in.1, bf16[128,4096]{1,0:T(8,128)(2,1)} %o_in.1, s32[1,128]{1,0:T(1,128)} %bitcast.1), custom_call_target="tpu_custom_call" | custom-call | flops 2700000000 | bytes 4000000 | tf_op jit(solution)/shard_map/pallas_call | solution.py:413
  25.3 2.1 %shard_map.77 = (bf16[128,4096]{1,0:T(8,128)(2,1)}, bf16[128,512]{1,0:T(8,128)(2,1)}, bf16[128,512]{1,0:T(8,128)(2,1)}) custom-call(bf16[128,4096]{1,0:T(8,128)(2,1)} %get-tuple-element.6.dq, bf16[128,512]{1,0:T(8,128)(2,1)} %get-tuple-element.7.dk, bf16[128,512]{1,0:T(8,128)(2,1)} %get-tuple-element.8.dv), custom_call_target="tpu_custom_call" | custom-call | tf_op jit(solution)/shard_map/pallas_call | solution.py:453

commit v8 on v7

--- a/solution.py
+++ b/solution.py
@@ -336,8 +336,8 @@
     wait_side()
     wait_near(0)
     send_far(0)
+    unit(0, 1, True, lambda: None)
     send_near(1)
-    unit(0, 1, True, lambda: None)
     send_far(1)
     wait_far(0)
     unit(0, 0, False, lambda: send_back(0, (0, 1, 2, 3)))

time: 27.9 us -> 28 us (level); the launches traced: 27.5 us -> 27.9 us
  Pallas kernels: 26.9 us -> 27.3 us
    pallas_call x1, Pallas kernels: 24.7 us -> 25.1 us  [body(): pl.pallas_call(functools.partial(kernel, inner, count), out_shape=(jax.Sh...]
where the time goes in v8:
time: 28 us; the launch traced here: 27.9 us
  Pallas kernels  27.3 us (98%)
  between operations  0.64 us (2%)
    pallas_call x1, Pallas kernels, body(): pl.pallas_call(functools.partial(kernel, inner, count), out_shape=(jax.Sh...  25.1 us
    pallas_call x1, Pallas kernels, body(): pl.pallas_call(finish, out_shape=tuple((jax.ShapeDtypeStruct(part.shape,...  2.15 us

profile of v8, /device:TPU:7, one launch (start us, length us, event | category | flops | bytes accessed | tf_op | source)
XLA Modules:
  0.0 27.9 jit_solution(14699622254523445738)
XLA Ops:
  0.6 25.1 %shard_map.76 = (bf16[128,4096]{1,0:T(8,128)(2,1)}, bf16[128,512]{1,0:T(8,128)(2,1)}, bf16[128,512]{1,0:T(8,128)(2,1)}) custom-call(bf16[128,4096]{1,0:T(8,128)(2,1)} %q_in.1, bf16[128,512]{1,0:T(8,128)(2,1)} %k_in.1, bf16[128,512]{1,0:T(8,128)(2,1)} %v_in.1, bf16[128,4096]{1,0:T(8,128)(2,1)} %o_in.1, s32[1,128]{1,0:T(1,128)} %bitcast.1), custom_call_target="tpu_custom_call" | custom-call | flops 2700000000 | bytes 4000000 | tf_op jit(solution)/shard_map/pallas_call | solution.py:413
  25.7 2.1 %shard_map.77 = (bf16[128,4096]{1,0:T(8,128)(2,1)}, bf16[128,512]{1,0:T(8,128)(2,1)}, bf16[128,512]{1,0:T(8,128)(2,1)}) custom-call(bf16[128,4096]{1,0:T(8,128)(2,1)} %get-tuple-element.6.dq, bf16[128,512]{1,0:T(8,128)(2,1)} %get-tuple-element.7.dk, bf16[128,512]{1,0:T(8,128)(2,1)} %get-tuple-element.8.dv), custom_call_target="tpu_custom_call" | custom-call | tf_op jit(solution)/shard_map/pallas_call | solution.py:453
